TPU v7x, 256 devices: a whole 4x4x8 slice. The times are simulated.
256 devices in a mesh: rep: 64 (over z, y, core), shard: 4 (over x).
Axes of the slice: x: 4, y: 4, z: 8, core: 2. Of those that a mesh axis runs over, the one named last changes fastest.
Arguments:
- grad_parts: bfloat16 [64, 4, 64, 28672], P('rep', 'shard'), may hold values from -6 to 6
- momentum: float32 [64, 64, 28672], P('rep', None, 'shard')
- indices: int32 [64, 1, 448, 32], P(None, None, 'shard'), may hold values from 0 to 4095, as said below
Outputs:
- momentum_next: float32 [64, 64, 28672], P('rep', None, 'shard')
- update: float32 [64, 28672], P(None, 'shard')
Inputs may be any that keep to these rules, and one draw needn't show every extreme that they name: `indices`: within each list the 32 positions are distinct.
All inputs are finite; a program needn't handle non-finite values.
Results may differ from a plain program's by a relative error of at most 0.0003.
Values sent between devices are 32-bit elements; how exact they have to be, the bound alone decides.
A program may use at most 64 MiB of HBM per device.

v0:
```python
import jax
import jax.numpy as jnp
from jax import lax
from jax.sharding import PartitionSpec as P

STRETCH = 64


momentum_decay = 0.9


def stretch_table():
    size = STRETCH
    freq = jnp.arange(size, dtype=jnp.float32)[:, None]
    place = jnp.arange(size, dtype=jnp.float32)[None, :]
    weights = jnp.where(freq == 0.0, jnp.sqrt(1.0 / size), jnp.sqrt(2.0 / size)).astype(jnp.float32)
    return weights * jnp.cos(jnp.pi * (2.0 * place + 1.0) * freq / (2.0 * size))


def forward_stretches(field, table):
    rows, cols = field.shape
    blocks = field.reshape(rows // STRETCH, STRETCH, cols // STRETCH, STRETCH)
    first = jnp.einsum("ka,iajb->ikjb", table, blocks, precision=lax.Precision.HIGHEST)
    second = jnp.einsum("ikjb,lb->ijkl", first, table, precision=lax.Precision.HIGHEST)
    return second


def inverse_stretches(square, table):
    row_blocks, col_blocks, _, _ = square.shape
    first = jnp.einsum("ka,ijkl->ijal", table, square, precision=lax.Precision.HIGHEST)
    second = jnp.einsum("ijal,lb->iajb", first, table, precision=lax.Precision.HIGHEST)
    return second.reshape(row_blocks * STRETCH, col_blocks * STRETCH)


def split_hot(positions):
    levels = jnp.arange(STRETCH, dtype=jnp.int32)
    row_part = (positions // STRETCH)[..., None] == levels
    col_part = (positions % STRETCH)[..., None] == levels
    return (row_part.astype(jnp.float32), col_part.astype(jnp.float32))


def pick_values(square, positions):
    row_hot, col_hot = split_hot(positions)
    rows_taken = jnp.einsum("ijmk,ijkl->ijml", row_hot, square, precision=lax.Precision.HIGHEST)
    return jnp.sum(rows_taken * col_hot, axis=3)


def spread_many(values, positions):
    row_hot, col_hot = split_hot(positions)
    return jnp.einsum(
        "gijmk,gijml->ijkl", row_hot * values[..., None], col_hot, precision=lax.Precision.HIGHEST
    )


def body(grad_parts, momentum, indices):
    table = stretch_table()
    partial_value = grad_parts[0, 0].astype(jnp.float32)
    gradient = lax.psum_scatter(partial_value, "shard", scatter_dimension=1, tiled=True)
    accumulated = momentum_decay * momentum[0] + gradient
    rows, cols = accumulated.shape
    row_blocks = rows // STRETCH
    col_blocks = cols // STRETCH
    square = forward_stretches(accumulated, table)
    chosen = lax.dynamic_index_in_dim(indices, lax.axis_index("rep"), 0, keepdims=False)
    kept = pick_values(square, chosen)
    own = spread_many(kept[None], chosen[None])
    replicas = lax.axis_size("rep")
    every_kept = lax.all_gather(kept[None], "rep", axis=0, tiled=True)
    group = min(8, replicas)
    rounds = replicas // group
    grouped_values = every_kept.reshape((rounds, group) + kept.shape)
    grouped_places = indices.reshape((rounds, group) + chosen.shape)

    def add_group(carry, pieces):
        return (carry + spread_many(pieces[0], pieces[1]), None)

    start = jnp.zeros(own.shape, jnp.float32)
    total, _ = lax.scan(add_group, start, (grouped_values, grouped_places))
    moment_next = accumulated - inverse_stretches(own, table)
    decoded = inverse_stretches(total / replicas, table)
    blocks = decoded.reshape(row_blocks, STRETCH, col_blocks, STRETCH)
    squares = jnp.mean(blocks * blocks, axis=(1, 3), keepdims=True)
    update = (blocks / jnp.sqrt(squares + 1e-06)).reshape(rows, cols)
    return (moment_next[None], update)


def solution(mesh):
    in_specs = (
        P("rep", "shard", None, None),
        P("rep", None, "shard"),
        P(None, None, "shard", None),
    )
    out_specs = (P("rep", None, "shard"), P(None, "shard"))
    return jax.shard_map(body, mesh=mesh, in_specs=in_specs, out_specs=out_specs, check_vma=False)
```

profile of v0, /device:TPU:1, one launch (start us, length us, event | category | flops | bytes accessed | tf_op | source)
XLA Modules:
  0.0 487.0 jit_solution(9575682741336721587)
XLA Ops:
  7.2 5.5 %bitcast_convert_fusion = f32[64,28672]{1,0:T(8,128)} fusion(bf16[1,1,64,28672]{3,2,1,0:T(8,128)(2,1)} %param.5), kind=kLoop, calls=%fused_computation.22 | loop fusion | flops 1835008 | bytes 11010048 | tf_op jit(solution)/shard_map/convert_element_type | solution.py:57
  16.1 75.7 %reduce-scatter.2.cloned.1.call-done = f32[64,7168]{1,0:T(8,128)} async-done(((f32[64,28672]{1,0:T(8,128)}), f32[64,7168]{1,0:T(8,128)}) %reduce-scatter.2.cloned.1.call-update) | async-done | bytes 1835024 | tf_op jit(solution)/shard_map/reduce_scatter | solution.py:58
  108.7 5.1 %copy.39 = f32[112,64,64]{2,1,0:T(8,128)} copy(f32[112,64,64]{0,2,1:T(8,128)} %fusion.23) | data formatting | bytes 3670016 | tf_op jit(solution)/shard_map/reshape.25
  117.8 6.7 %fusion.20 = f32[112,64,64]{2,1,0:T(8,128)} fusion(s32[112,32]{1,0:T(8,128)S(1)} %copy.40, f32[112,32]{1,0:T(8,128)S(1)} %select_reduce_fusion, s32[112,32]{1,0:T(8,128)S(1)} %copy.32), kind=kOutput, calls=%fused_computation.37 | convolution fusion | flops 176848896 | bytes 1878016 | tf_op jit(solution)/shard_map/gijmk,gijml->ijkl/dot_general | solution.py:50
  124.5 5.0 %copy.41 = f32[112,64,64]{0,1,2:T(8,128)} copy(f32[112,64,64]{2,1,0:T(8,128)} %fusion.20) | data formatting | bytes 3670016 | tf_op jit(solution)/shard_map/gijmk,gijml->ijkl/dot_general | solution.py:50
  133.3 4.6 fusion.26
  147.9 51.8 %all-gather.1 = f32[64,112,32]{1,2,0:T(8,128)S(1)} all-gather(f32[1,112,32]{1,2,0:T(8,128)S(1)} %copy.44), channel_id=2, replica_groups=mesh['rep'=64,'shard'=4] {'rep'}, dimensions={0}, use_global_device_ids=true | all-gather | bytes 931840 | tf_op jit(solution)/shard_map/all_gather | solution.py:68
  199.7 259.9 %while.13 = (s32[]{:T(128)}, f32[1,112,64,64]{3,2,1,0:T(8,128)}, s32[8,8,1,112,32]{3,4,2,1,0:T(8,128)}, f32[8,8,1,112,32]{3,4,2,1,0:T(8,128)S(1)}, s32[]{:T(128)}, /*index=5*/s32[]{:T(128)}) while((s32[]{:T(128)}, f32[1,112,64,64]{3,2,1,0:T(8,128)}, s32[8,8,1,112,32]{3,4,2,1,0:T(8,128)}, f32[8,8,1,112,32]{3,4,2,1,0:T(8,128)S(1)}, ...), condition=%wide.region_3.4_spmd.clone, body=%wide.region_2.3_spmd.clone.sunk | while | flops 1416253440 | bytes 34635928 | solution.py:78
  201.6 7.8 %fusion.86 = f32[8,112,32,64]{3,2,0,1:T(8,128)S(1)} fusion(f32[8,112,32]{2,0,1:T(8,128)S(1)} %bitcast.143, s32[8,112,32]{2,0,1:T(8,128)S(1)} %get-tuple-element.128), kind=kLoop, calls=%fused_computation.2.clone.clone.clone.2.clone.1 | loop fusion | flops 3670016 | bytes 7569408 | tf_op jit(solution)/shard_map/while/body/eval_jaxpr/gijmk,gijml->ijkl/dot_general | solution.py:50
  209.5 20.9 %bitcast_add_fusion.3 = f32[1,112,64,64]{3,2,1,0:T(8,128)S(1)} fusion(f32[1,112,64,64]{3,2,1,0:T(8,128)S(1)} %copy-done, s32[8,112,32]{2,0,1:T(8,128)S(1)} %get-tuple-element.127, pred[]{:T(512)S(6)} %compare.37, f32[8,112,32,64]{3,2,0,1:T(8,128)S(1)} %fusion.86), kind=kOutput, calls=%fused_computation.8.clone.3 | convolution fusion | flops 1412038656 | bytes 11124737 | tf_op jit(solution)/shard_map/while/body/eval_jaxpr/gijmk,gijml->ijkl/dot_general | solution.py:50
  234.1 7.8 %fusion.86 = f32[8,112,32,64]{3,2,0,1:T(8,128)S(1)} fusion(f32[8,112,32]{2,0,1:T(8,128)S(1)} %bitcast.143, s32[8,112,32]{2,0,1:T(8,128)S(1)} %get-tuple-element.128), kind=kLoop, calls=%fused_computation.2.clone.clone.clone.2.clone.1 | loop fusion | flops 3670016 | bytes 7569408 | tf_op jit(solution)/shard_map/while/body/eval_jaxpr/gijmk,gijml->ijkl/dot_general | solution.py:50
  242.0 20.9 %bitcast_add_fusion.3 = f32[1,112,64,64]{3,2,1,0:T(8,128)S(1)} fusion(f32[1,112,64,64]{3,2,1,0:T(8,128)S(1)} %copy-done, s32[8,112,32]{2,0,1:T(8,128)S(1)} %get-tuple-element.127, pred[]{:T(512)S(6)} %compare.37, f32[8,112,32,64]{3,2,0,1:T(8,128)S(1)} %fusion.86), kind=kOutput, calls=%fused_computation.8.clone.3 | convolution fusion | flops 1412038656 | bytes 11124737 | tf_op jit(solution)/shard_map/while/body/eval_jaxpr/gijmk,gijml->ijkl/dot_general | solution.py:50
  266.6 7.8 %fusion.86 = f32[8,112,32,64]{3,2,0,1:T(8,128)S(1)} fusion(f32[8,112,32]{2,0,1:T(8,128)S(1)} %bitcast.143, s32[8,112,32]{2,0,1:T(8,128)S(1)} %get-tuple-element.128), kind=kLoop, calls=%fused_computation.2.clone.clone.clone.2.clone.1 | loop fusion | flops 3670016 | bytes 7569408 | tf_op jit(solution)/shard_map/while/body/eval_jaxpr/gijmk,gijml->ijkl/dot_general | solution.py:50
  274.4 20.9 %bitcast_add_fusion.3 = f32[1,112,64,64]{3,2,1,0:T(8,128)S(1)} fusion(f32[1,112,64,64]{3,2,1,0:T(8,128)S(1)} %copy-done, s32[8,112,32]{2,0,1:T(8,128)S(1)} %get-tuple-element.127, pred[]{:T(512)S(6)} %compare.37, f32[8,112,32,64]{3,2,0,1:T(8,128)S(1)} %fusion.86), kind=kOutput, calls=%fused_computation.8.clone.3 | convolution fusion | flops 1412038656 | bytes 11124737 | tf_op jit(solution)/shard_map/while/body/eval_jaxpr/gijmk,gijml->ijkl/dot_general | solution.py:50
  299.0 7.8 %fusion.86 = f32[8,112,32,64]{3,2,0,1:T(8,128)S(1)} fusion(f32[8,112,32]{2,0,1:T(8,128)S(1)} %bitcast.143, s32[8,112,32]{2,0,1:T(8,128)S(1)} %get-tuple-element.128), kind=kLoop, calls=%fused_computation.2.clone.clone.clone.2.clone.1 | loop fusion | flops 3670016 | bytes 7569408 | tf_op jit(solution)/shard_map/while/body/eval_jaxpr/gijmk,gijml->ijkl/dot_general | solution.py:50
  306.9 20.9 %bitcast_add_fusion.3 = f32[1,112,64,64]{3,2,1,0:T(8,128)S(1)} fusion(f32[1,112,64,64]{3,2,1,0:T(8,128)S(1)} %copy-done, s32[8,112,32]{2,0,1:T(8,128)S(1)} %get-tuple-element.127, pred[]{:T(512)S(6)} %compare.37, f32[8,112,32,64]{3,2,0,1:T(8,128)S(1)} %fusion.86), kind=kOutput, calls=%fused_computation.8.clone.3 | convolution fusion | flops 1412038656 | bytes 11124737 | tf_op jit(solution)/shard_map/while/body/eval_jaxpr/gijmk,gijml->ijkl/dot_general | solution.py:50
  331.5 7.8 %fusion.86 = f32[8,112,32,64]{3,2,0,1:T(8,128)S(1)} fusion(f32[8,112,32]{2,0,1:T(8,128)S(1)} %bitcast.143, s32[8,112,32]{2,0,1:T(8,128)S(1)} %get-tuple-element.128), kind=kLoop, calls=%fused_computation.2.clone.clone.clone.2.clone.1 | loop fusion | flops 3670016 | bytes 7569408 | tf_op jit(solution)/shard_map/while/body/eval_jaxpr/gijmk,gijml->ijkl/dot_general | solution.py:50
  339.4 20.9 %bitcast_add_fusion.3 = f32[1,112,64,64]{3,2,1,0:T(8,128)S(1)} fusion(f32[1,112,64,64]{3,2,1,0:T(8,128)S(1)} %copy-done, s32[8,112,32]{2,0,1:T(8,128)S(1)} %get-tuple-element.127, pred[]{:T(512)S(6)} %compare.37, f32[8,112,32,64]{3,2,0,1:T(8,128)S(1)} %fusion.86), kind=kOutput, calls=%fused_computation.8.clone.3 | convolution fusion | flops 1412038656 | bytes 11124737 | tf_op jit(solution)/shard_map/while/body/eval_jaxpr/gijmk,gijml->ijkl/dot_general | solution.py:50
  364.0 7.8 %fusion.86 = f32[8,112,32,64]{3,2,0,1:T(8,128)S(1)} fusion(f32[8,112,32]{2,0,1:T(8,128)S(1)} %bitcast.143, s32[8,112,32]{2,0,1:T(8,128)S(1)} %get-tuple-element.128), kind=kLoop, calls=%fused_computation.2.clone.clone.clone.2.clone.1 | loop fusion | flops 3670016 | bytes 7569408 | tf_op jit(solution)/shard_map/while/body/eval_jaxpr/gijmk,gijml->ijkl/dot_general | solution.py:50
  371.8 20.9 %bitcast_add_fusion.3 = f32[1,112,64,64]{3,2,1,0:T(8,128)S(1)} fusion(f32[1,112,64,64]{3,2,1,0:T(8,128)S(1)} %copy-done, s32[8,112,32]{2,0,1:T(8,128)S(1)} %get-tuple-element.127, pred[]{:T(512)S(6)} %compare.37, f32[8,112,32,64]{3,2,0,1:T(8,128)S(1)} %fusion.86), kind=kOutput, calls=%fused_computation.8.clone.3 | convolution fusion | flops 1412038656 | bytes 11124737 | tf_op jit(solution)/shard_map/while/body/eval_jaxpr/gijmk,gijml->ijkl/dot_general | solution.py:50
  396.4 7.8 %fusion.86 = f32[8,112,32,64]{3,2,0,1:T(8,128)S(1)} fusion(f32[8,112,32]{2,0,1:T(8,128)S(1)} %bitcast.143, s32[8,112,32]{2,0,1:T(8,128)S(1)} %get-tuple-element.128), kind=kLoop, calls=%fused_computation.2.clone.clone.clone.2.clone.1 | loop fusion | flops 3670016 | bytes 7569408 | tf_op jit(solution)/shard_map/while/body/eval_jaxpr/gijmk,gijml->ijkl/dot_general | solution.py:50
  404.3 20.9 %bitcast_add_fusion.3 = f32[1,112,64,64]{3,2,1,0:T(8,128)S(1)} fusion(f32[1,112,64,64]{3,2,1,0:T(8,128)S(1)} %copy-done, s32[8,112,32]{2,0,1:T(8,128)S(1)} %get-tuple-element.127, pred[]{:T(512)S(6)} %compare.37, f32[8,112,32,64]{3,2,0,1:T(8,128)S(1)} %fusion.86), kind=kOutput, calls=%fused_computation.8.clone.3 | convolution fusion | flops 1412038656 | bytes 11124737 | tf_op jit(solution)/shard_map/while/body/eval_jaxpr/gijmk,gijml->ijkl/dot_general | solution.py:50
  428.9 7.8 %fusion.86 = f32[8,112,32,64]{3,2,0,1:T(8,128)S(1)} fusion(f32[8,112,32]{2,0,1:T(8,128)S(1)} %bitcast.143, s32[8,112,32]{2,0,1:T(8,128)S(1)} %get-tuple-element.128), kind=kLoop, calls=%fused_computation.2.clone.clone.clone.2.clone.1 | loop fusion | flops 3670016 | bytes 7569408 | tf_op jit(solution)/shard_map/while/body/eval_jaxpr/gijmk,gijml->ijkl/dot_general | solution.py:50
  436.8 20.9 %bitcast_add_fusion.3 = f32[1,112,64,64]{3,2,1,0:T(8,128)S(1)} fusion(f32[1,112,64,64]{3,2,1,0:T(8,128)S(1)} %copy-done, s32[8,112,32]{2,0,1:T(8,128)S(1)} %get-tuple-element.127, pred[]{:T(512)S(6)} %compare.37, f32[8,112,32,64]{3,2,0,1:T(8,128)S(1)} %fusion.86), kind=kOutput, calls=%fused_computation.8.clone.3 | convolution fusion | flops 1412038656 | bytes 11124737 | tf_op jit(solution)/shard_map/while/body/eval_jaxpr/gijmk,gijml->ijkl/dot_general | solution.py:50
  (103 shorter events, 87.9 us)
Async XLA Ops:
  7.2 84.6 %reduce-scatter.2.cloned.1.call-start = ((), (), s32[]{:S(2)}) async-start(), calls=%async_computation.1 | async-start | bytes 9175040 | tf_op jit(solution)/shard_map/reduce_scatter | solution.py:58
  201.6 7.9 %copy-start = (f32[1,112,64,64]{3,2,1,0:T(8,128)S(1)}, f32[1,112,64,64]{3,2,1,0:T(8,128)}, u32[]{:S(2)}) copy-start(f32[1,112,64,64]{3,2,1,0:T(8,128)} %get-tuple-element.136) | copy-start | bytes 5505028 | tf_op jit(solution)/shard_map/while
  230.4 1.9 copy-start.1
  234.1 7.9 %copy-start = (f32[1,112,64,64]{3,2,1,0:T(8,128)S(1)}, f32[1,112,64,64]{3,2,1,0:T(8,128)}, u32[]{:S(2)}) copy-start(f32[1,112,64,64]{3,2,1,0:T(8,128)} %get-tuple-element.136) | copy-start | bytes 5505028 | tf_op jit(solution)/shard_map/while
  262.8 1.9 copy-start.1
  266.5 7.9 %copy-start = (f32[1,112,64,64]{3,2,1,0:T(8,128)S(1)}, f32[1,112,64,64]{3,2,1,0:T(8,128)}, u32[]{:S(2)}) copy-start(f32[1,112,64,64]{3,2,1,0:T(8,128)} %get-tuple-element.136) | copy-start | bytes 5505028 | tf_op jit(solution)/shard_map/while
  295.3 1.9 copy-start.1
  299.0 7.9 %copy-start = (f32[1,112,64,64]{3,2,1,0:T(8,128)S(1)}, f32[1,112,64,64]{3,2,1,0:T(8,128)}, u32[]{:S(2)}) copy-start(f32[1,112,64,64]{3,2,1,0:T(8,128)} %get-tuple-element.136) | copy-start | bytes 5505028 | tf_op jit(solution)/shard_map/while
  327.8 1.9 copy-start.1
  331.5 7.9 %copy-start = (f32[1,112,64,64]{3,2,1,0:T(8,128)S(1)}, f32[1,112,64,64]{3,2,1,0:T(8,128)}, u32[]{:S(2)}) copy-start(f32[1,112,64,64]{3,2,1,0:T(8,128)} %get-tuple-element.136) | copy-start | bytes 5505028 | tf_op jit(solution)/shard_map/while
  360.2 1.9 copy-start.1
  363.9 7.9 %copy-start = (f32[1,112,64,64]{3,2,1,0:T(8,128)S(1)}, f32[1,112,64,64]{3,2,1,0:T(8,128)}, u32[]{:S(2)}) copy-start(f32[1,112,64,64]{3,2,1,0:T(8,128)} %get-tuple-element.136) | copy-start | bytes 5505028 | tf_op jit(solution)/shard_map/while
  392.7 1.9 copy-start.1
  396.4 7.9 %copy-start = (f32[1,112,64,64]{3,2,1,0:T(8,128)S(1)}, f32[1,112,64,64]{3,2,1,0:T(8,128)}, u32[]{:S(2)}) copy-start(f32[1,112,64,64]{3,2,1,0:T(8,128)} %get-tuple-element.136) | copy-start | bytes 5505028 | tf_op jit(solution)/shard_map/while
  425.2 1.9 copy-start.1
  428.9 7.9 %copy-start = (f32[1,112,64,64]{3,2,1,0:T(8,128)S(1)}, f32[1,112,64,64]{3,2,1,0:T(8,128)}, u32[]{:S(2)}) copy-start(f32[1,112,64,64]{3,2,1,0:T(8,128)} %get-tuple-element.136) | copy-start | bytes 5505028 | tf_op jit(solution)/shard_map/while
  457.6 1.9 copy-start.1
Sparse Core Ops, SparseCore 0:
  12.8 78.8 reduce-scatter.1
where the time goes:
time: 488 us; the launch traced here: 487 us
  matrix products  200 us (41%)
  other arithmetic  84.2 us (17%)
  waiting for transfers between devices  75.7 us (16%)
  local copies, waits for them, and re-layouts  60.4 us (12%)
  blocking collectives  51.8 us (11%)
  between operations  14.1 us (3%)
    dot_general x9, matrix products, spread_many(): jnp.einsum('gijmk,gijml->ijkl', row_hot * values[..., None], col_hot, pre...  174 us
    reduce_scatter x1, waiting for transfers between devices, body(): lax.psum_scatter(partial_value, 'shard', scatter_dimension=1, tiled=True)  75.7 us
    dot_general x8, other arithmetic, spread_many(): jnp.einsum('gijmk,gijml->ijkl', row_hot * values[..., None], col_hot, pre...  62.8 us
    all_gather x1, blocking collectives, body(): every_kept = lax.all_gather(kept[None], 'rep', axis=0, tiled=True)  51.8 us
    another operation x4, local copies, waits for them, and re-layouts  15.7 us
    while x32, local copies, waits for them, and re-layouts  15.2 us
    dynamic_slice x32, local copies, waits for them, and re-layouts, body(): total, _ = lax.scan(add_group, start, (grouped_values, grouped_places))  10.9 us
  transfers between devices with their start and end apart: 1, of which 1 were waited for; matrix products, arithmetic and copies ran while one was open for 1% of the time, Pallas kernels for 0%

commit v1 on v0

v1 whole, which is shorter than its diff:
```python
import functools

import jax
import jax.numpy as jnp
import numpy as np
from jax import lax
from jax.experimental import pallas as pl
from jax.experimental.pallas import tpu as pltpu
from jax.sharding import PartitionSpec as P

MESH = pl.DeviceIdType.MESH
F32, BF16, I32 = jnp.float32, jnp.bfloat16, jnp.int32

SIDE = 64
KEEP = 32
NX = 4
NY = 4
NC = 2
BLOCKS = 8
WIDTH = BLOCKS * SIDE
QUAD = 4 * SIDE
DECAY = 0.9


def tables():
    freq = np.arange(SIDE, dtype=np.float64)[:, None]
    place = np.arange(SIDE, dtype=np.float64)[None, :]
    weight = np.where(freq == 0, np.sqrt(1.0 / SIDE), np.sqrt(2.0 / SIDE))
    table = (weight * np.cos(np.pi * (2 * place + 1) * freq / (2 * SIDE))).astype(np.float32)
    high = table.astype(BF16)
    low = (table - high.astype(np.float32)).astype(BF16)
    four = np.eye(4)

    def spread(x):
        return np.kron(four, x.astype(np.float32)).astype(BF16)

    return np.concatenate(
        [
            np.concatenate([high, low, high, low], axis=1),
            np.concatenate([high.T, low.T, high.T, low.T], axis=1),
            spread(high.T),
            spread(low.T),
            spread(high),
            spread(low),
            spread(np.ones((SIDE, SIDE))),
        ],
        axis=0,
    )


ROWS_LEFT, ROWS_LEFT_T = (0, 64), (64, 128)
ROWS_FWD_H, ROWS_FWD_L = (128, 384), (384, 640)
ROWS_INV_H, ROWS_INV_L = (640, 896), (896, 1152)
ROWS_ONES = (1152, 1408)


def two(x):
    high = x.astype(BF16)
    return high, (x - high.astype(F32)).astype(BF16)


def dot(a, b):
    return jnp.dot(a, b, preferred_element_type=F32)


def right(x, high, low):
    xh, xl = two(x)
    stack = jnp.concatenate([xh[:, :QUAD], xh[:, QUAD:], xl[:, :QUAD], xl[:, QUAD:]], axis=0)
    p = dot(stack, high)
    q = dot(stack[: 2 * SIDE], low)
    s = p[: 2 * SIDE] + p[2 * SIDE :] + q
    return jnp.concatenate([s[:SIDE], s[SIDE:]], axis=1)


def stacked(y):
    yh, yl = two(y)
    return jnp.concatenate([yh, yh, yl, yl], axis=0)


def kernel(
    groups, grad_hbm, mom_hbm, idx_hbm, tab_hbm, next_hbm, upd_hbm,
    grad_v, mom_v, idx_v, tab_v, own_fwd, own_raw, got_fwd, got, next_v, upd_v, y_buf, z_buf, k_buf, l_buf, h_buf, w_buf, s_buf,
    in_sem, mom_sem, idx_sem, tab_sem, fwd_send, raw_send, sum_send, fwd_recv, got_recv, y_send, y_recv, z_send, z_recv, out_sem,
):
    width = groups * WIDTH
    half = SIDE // 2
    x = lax.axis_index("shard")
    rep = lax.axis_index("rep")
    nz = lax.axis_size("rep") // (NY * NC)
    z, y, c = rep // (NY * NC), (rep // NC) % NY, rep % NC
    left, right_x, far = (x + NX - 1) % NX, (x + 1) % NX, (x + 2) % NX
    place = y * NC + c

    def rep_of(z_, place_):
        return z_ * (NY * NC) + place_

    def load(g, which):
        d = (x + which) % NX
        return pltpu.make_async_copy(
            grad_hbm.at[:, pl.ds(pl.multiple_of(d * width + g * WIDTH, 128), WIDTH)],
            grad_v.at[which, g],
            in_sem.at[which, g],
        )

    def load_mom(g):
        return pltpu.make_async_copy(
            mom_hbm.at[:, pl.ds(pl.multiple_of(g * WIDTH, 128), WIDTH)], mom_v.at[g], mom_sem.at[g]
        )

    def start_loads(g):
        for which in (2, 3, 1, 0):
            load(g, which).start()
        load_mom(g).start()

    load_idx = pltpu.make_async_copy(idx_hbm, idx_v, idx_sem)
    load_tab = pltpu.make_async_copy(tab_hbm, tab_v, tab_sem)

    def to_x(src, dst, send, recv, where):
        return pltpu.make_async_remote_copy(
            src_ref=src, dst_ref=dst, send_sem=send, recv_sem=recv, device_id=(rep, where), device_id_type=MESH
        )

    def copy_fwd(g, way):
        return to_x(
            own_fwd.at[g, way], got_fwd.at[g, way], fwd_send, fwd_recv.at[g], left if way == 0 else right_x
        )

    def copy_raw(g, way):
        rows = pl.ds(half, half) if way == 0 else pl.ds(0, half)
        return to_x(
            own_raw.at[g, way], got.at[g, way, rows], raw_send, got_recv.at[g], left if way == 0 else right_x
        )

    def copy_sum(g, way):
        rows = pl.ds(0, half) if way == 0 else pl.ds(half, half)
        return to_x(
            own_fwd.at[groups + g, way], got.at[g, way, rows], sum_send, got_recv.at[g], left if way == 0 else right_x
        )

    def copy_y(g, step):
        other = (place + step) % (NY * NC)
        return pltpu.make_async_remote_copy(
            src_ref=y_buf.at[g, 0],
            dst_ref=y_buf.at[g, NY * NC - step],
            send_sem=y_send,
            recv_sem=y_recv.at[g],
            device_id=(rep_of(z, other), x),
            device_id_type=MESH,
        )

    def copy_z(g, step):
        other = (z + step) % nz
        return pltpu.make_async_remote_copy(
            src_ref=z_buf.at[g, 0],
            dst_ref=z_buf.at[g, nz - step],
            send_sem=z_send,
            recv_sem=z_recv.at[g],
            device_id=(rep_of(other, place), x),
            device_id_type=MESH,
        )

    def drain(ref, sem):
        pltpu.make_async_copy(ref, ref, sem).wait()

    def stage_a(g):
        for which in (2, 3, 1, 0):
            load(g, which).wait()
        own_fwd[g, 0] = grad_v[2, g, :half].astype(F32)
        copy_fwd(g, 0).start()
        own_fwd[g, 1] = grad_v[2, g, half:].astype(F32)
        copy_fwd(g, 1).start()
        own_raw[g, 0] = grad_v[3, g, half:].astype(F32)
        copy_raw(g, 0).start()
        own_raw[g, 1] = grad_v[1, g, :half].astype(F32)
        copy_raw(g, 1).start()

    def stage_b(g):
        drain(got_fwd.at[g], fwd_recv.at[g])
        own_fwd[groups + g, 0] = grad_v[3, g, :half].astype(F32) + got_fwd[g, 0]
        copy_sum(g, 0).start()
        own_fwd[groups + g, 1] = grad_v[1, g, half:].astype(F32) + got_fwd[g, 1]
        copy_sum(g, 1).start()

    def tab(rows):
        return tab_v[rows[0] : rows[1], :]

    def stage_c(g):
        mine = idx_v[rep, g]
        spread = jnp.broadcast_to(mine[:, None, :], (BLOCKS, KEEP, KEEP)).reshape(BLOCKS * KEEP, KEEP)
        row = lax.broadcasted_iota(I32, (BLOCKS * KEEP, KEEP), 0)
        lane = lax.broadcasted_iota(I32, (BLOCKS * KEEP, KEEP), 1)
        flat = jnp.sum(jnp.where(row % KEEP == lane, spread, 0), axis=1, keepdims=True)
        row_of, col_of = flat // SIDE, flat % SIDE
        row_hot = jnp.where(lax.broadcasted_iota(I32, (BLOCKS * KEEP, SIDE), 1) == row_of, 1.0, 0.0).astype(BF16)
        taken = dot(row_hot, tab(ROWS_LEFT)).astype(BF16)
        block_of = lax.broadcasted_iota(I32, (BLOCKS * KEEP, 1), 0) // KEEP
        hit = lax.broadcasted_iota(I32, (BLOCKS * KEEP, WIDTH), 1) == block_of * SIDE + col_of
        drain(got.at[g], got_recv.at[g])
        load_mom(g).wait()
        acc = DECAY * mom_v[g] + (grad_v[0, g].astype(F32) + (got[g, 0] + got[g, 1]))
        first = right(acc, tab(ROWS_FWD_H), tab(ROWS_FWD_L))
        rows_taken = dot(taken, stacked(first))
        kept = jnp.where(hit, rows_taken, 0.0)
        column = jnp.sum(kept, axis=1, keepdims=True)
        slot = lax.broadcasted_iota(I32, (BLOCKS * KEEP, 128), 0) % KEEP + y * KEEP
        lanes = jnp.where(lax.broadcasted_iota(I32, (BLOCKS * KEEP, 128), 1) == slot, column, 0.0)
        y_buf[g, 0] = jnp.sum(lanes.reshape(BLOCKS, KEEP, 128), axis=1)
        for step in range(1, NY * NC):
            copy_y(g, step).start()
        kh, kl = two(kept)
        both = taken[:, : 2 * SIDE]
        dims = (((0,), (0,)), ((), ()))
        back = lax.dot_general(both, kh, dims, preferred_element_type=F32)
        back += lax.dot_general(both, kl, dims, preferred_element_type=F32)
        next_v[g] = acc - right(back[:SIDE] + back[SIDE:], tab(ROWS_INV_H), tab(ROWS_INV_L))
        write_out(g, next_v, next_hbm, 0).start()

    def write_out(g, src, dst, which):
        return pltpu.make_async_copy(
            src.at[g], dst.at[:, pl.ds(pl.multiple_of(g * WIDTH, 128), WIDTH)], out_sem.at[which, g]
        )

    def stage_d(g):
        drain(y_buf.at[g, pl.ds(1, NY * NC - 1)], y_recv.at[g])
        for core in range(NC):
            same = (core + NC - c) % NC
            total = y_buf[g, same]
            for step in range(1, NY):
                total += y_buf[g, same + NC * step]
            z_buf[g, 0, core] = total
        for step in range(1, nz):
            copy_z(g, step).start()

    def stage_e(g):
        for t in range(nz):
            other = (z + t) % nz
            for core in range(NC):
                flat = jnp.concatenate([idx_v[rep_of(other, q * NC + core), g] for q in range(NY)], axis=1)
                k_buf[t, core] = flat // SIDE
                l_buf[t, core] = flat % SIDE
        drain(z_buf.at[g, pl.ds(1, nz - 1)], z_recv.at[g])
        value = z_buf[g]
        high = value.astype(BF16).astype(F32)
        h_buf[...] = high
        w_buf[...] = value - high
        level = lax.broadcasted_iota(I32, (SIDE, 128), 0)

        def one_block(j, carry):
            at = pl.ds(j, 1)
            lhs, rhs_h, rhs_l = [], [], []
            for t in range(nz):
                for core in range(NC):
                    in_row = level == k_buf[t, core, at, :]
                    in_col = level == l_buf[t, core, at, :]
                    lhs.append(jnp.where(in_row, 1.0, 0.0).astype(BF16))
                    rhs_h.append(jnp.where(in_col, h_buf[t, core, at, :], 0.0).astype(BF16))
                    rhs_l.append(jnp.where(in_col, w_buf[t, core, at, :], 0.0).astype(BF16))
            a = jnp.concatenate(lhs, axis=1)
            b = jnp.concatenate([jnp.concatenate(rhs_h, axis=1), jnp.concatenate(rhs_l, axis=1)], axis=0)
            s_buf[j] = lax.dot_general(a, b, (((1,), (1,)), ((), ())), preferred_element_type=F32)
            return carry

        lax.fori_loop(0, BLOCKS, one_block, 0)
        total = jnp.concatenate([s_buf[j, :, :SIDE] + s_buf[j, :, SIDE:] for j in range(BLOCKS)], axis=1)
        total = total * (1.0 / (nz * NY * NC))
        first = dot(tab(ROWS_LEFT_T), stacked(total))
        decoded = right(first, tab(ROWS_INV_H), tab(ROWS_INV_L))
        squares = jnp.sum(decoded * decoded, axis=0, keepdims=True)
        sh, sl = two(jnp.concatenate([squares[:, :QUAD], squares[:, QUAD:]] + [jnp.zeros((6, QUAD), F32)], axis=0))
        q = dot(sh, tab(ROWS_ONES)) + dot(sl, tab(ROWS_ONES))
        scale = 1.0 / jnp.sqrt(q * (1.0 / (SIDE * SIDE)) + 1e-6)
        upd_v[g] = decoded * jnp.concatenate([scale[0:1], scale[1:2]], axis=1)
        write_out(g, upd_v, upd_hbm, 1).start()

    start_loads(0)
    barrier = pltpu.get_barrier_semaphore()
    for where in (left, right_x):
        pl.semaphore_signal(barrier, inc=1, device_id=(rep, where), device_id_type=MESH)
    for step in range(1, NY * NC):
        pl.semaphore_signal(
            barrier, inc=1, device_id=(rep_of(z, (place + step) % (NY * NC)), x), device_id_type=MESH
        )
    for step in range(1, nz):
        pl.semaphore_signal(barrier, inc=1, device_id=(rep_of((z + step) % nz, place), x), device_id_type=MESH)
    start_loads(1)
    load_tab.start()
    load_idx.start()
    pl.semaphore_wait(barrier, 2 + NY * NC - 1 + nz - 1)

    def step(t, carry):
        def at(lag, stage):
            g = t - lag

            @pl.when((g >= 0) & (g < groups))
            def _():
                stage(g)

        @pl.when(t + 2 < groups)
        def _():
            start_loads(t + 2)

        at(0, stage_a)
        at(1, stage_b)

        @pl.when(t == 2)
        def _():
            load_tab.wait()
            load_idx.wait()

        at(2, stage_c)
        at(3, stage_d)
        at(4, stage_e)
        return carry

    lax.fori_loop(0, groups + 4, step, 0)

    drain(own_fwd.at[pl.ds(0, groups)], fwd_send)
    drain(own_fwd.at[pl.ds(groups, groups)], sum_send)
    drain(own_raw, raw_send)
    drain(y_buf.at[:, pl.ds(1, NY * NC - 1)], y_send)
    drain(z_buf.at[:, pl.ds(1, nz - 1)], z_send)

    def finish(g, carry):
        write_out(g, next_v, next_hbm, 0).wait()
        write_out(g, upd_v, upd_hbm, 1).wait()
        return carry

    lax.fori_loop(0, groups, finish, 0)


def body(grad_parts, momentum, indices):
    grad = grad_parts[0, 0]
    mom = momentum[0]
    rows, width = mom.shape
    groups = width // WIDTH
    reps = indices.shape[0]
    nz = reps // (NY * NC)
    idx = indices.reshape(reps, groups, BLOCKS, KEEP)
    half = SIDE // 2
    dma = pltpu.SemaphoreType.DMA
    any_space = pl.BlockSpec(memory_space=pl.ANY)
    scratch = [
        pltpu.VMEM((NX, groups, SIDE, WIDTH), BF16),
        pltpu.VMEM((groups, SIDE, WIDTH), F32),
        pltpu.VMEM((reps, groups, BLOCKS, KEEP), I32),
        pltpu.VMEM((1408, QUAD), BF16),
        pltpu.VMEM((2 * groups, 2, half, WIDTH), F32),
        pltpu.VMEM((groups, 2, half, WIDTH), F32),
        pltpu.VMEM((groups, 2, half, WIDTH), F32),
        pltpu.VMEM((groups, 2, SIDE, WIDTH), F32),
        pltpu.VMEM((groups, SIDE, WIDTH), F32),
        pltpu.VMEM((groups, SIDE, WIDTH), F32),
        pltpu.VMEM((groups, NY * NC, BLOCKS, 128), F32),
        pltpu.VMEM((groups, nz, NC, BLOCKS, 128), F32),
        pltpu.VMEM((nz, NC, BLOCKS, 128), I32),
        pltpu.VMEM((nz, NC, BLOCKS, 128), I32),
        pltpu.VMEM((nz, NC, BLOCKS, 128), F32),
        pltpu.VMEM((nz, NC, BLOCKS, 128), F32),
        pltpu.VMEM((BLOCKS, SIDE, 2 * SIDE), F32),
        dma((NX, groups)),
        dma((groups,)),
        dma,
        dma,
        dma,
        dma,
        dma,
        dma((groups,)),
        dma((groups,)),
        dma,
        dma((groups,)),
        dma,
        dma((groups,)),
        dma((2, groups)),
    ]
    out = jax.ShapeDtypeStruct((rows, width), F32)
    moment_next, update = pl.pallas_call(
        functools.partial(kernel, groups),
        out_shape=(out, out),
        in_specs=[any_space] * 4,
        out_specs=(any_space, any_space),
        scratch_shapes=scratch,
        compiler_params=pltpu.CompilerParams(
            collective_id=0, has_side_effects=True, vmem_limit_bytes=56 * 1024 * 1024
        ),
    )(grad, mom, idx, jnp.asarray(tables()))
    return (moment_next[None], update)


def solution(mesh):
    in_specs = (
        P("rep", "shard", None, None),
        P("rep", None, "shard"),
        P(None, None, "shard", None),
    )
    out_specs = (P("rep", None, "shard"), P(None, "shard"))
    return jax.shard_map(body, mesh=mesh, in_specs=in_specs, out_specs=out_specs, check_vma=False)
```

time: 488 us -> 111 us (0.23)
  matrix products: 200 us -> 0 us
  Pallas kernels: 0 us -> 103 us
  other arithmetic: 84.2 us -> 0 us
  waiting for transfers between devices: 75.7 us -> 0 us
  local copies, waits for them, and re-layouts: 60.4 us -> 7.61 us
  blocking collectives: 51.8 us -> 0 us
  between operations: 14.1 us -> 0.65 us
    dot_general x16 -> x0, matrix products: 200 us -> none  [the longest x9 174 us: spread_many(): jnp.einsum('gijmk,gijml->ijkl', row_hot * values[..., None], col_hot, pre...]
    pallas_call x0 -> x1, Pallas kernels: none -> 103 us  [body(): pl.pallas_call(functools.partial(kernel, groups), out_shape=(out, out), i...]
    reduce_scatter x1 -> x0, waiting for transfers between devices: 75.7 us -> none  [body(): lax.psum_scatter(partial_value, 'shard', scatter_dimension=1, tiled=True)]
    dot_general x8 -> x0, other arithmetic: 62.8 us -> none  [spread_many(): jnp.einsum('gijmk,gijml->ijkl', row_hot * values[..., None], col_hot, pre...]
    all_gather x1 -> x0, blocking collectives: 51.8 us -> none  [body(): every_kept = lax.all_gather(kept[None], 'rep', axis=0, tiled=True)]
    another operation x4 -> x0, local copies, waits for them, and re-layouts: 15.7 us -> none
    while x32 -> x0, local copies, waits for them, and re-layouts: 15.2 us -> none
    dynamic_slice x32 -> x0, local copies, waits for them, and re-layouts: 10.9 us -> none  [body(): total, _ = lax.scan(add_group, start, (grouped_values, grouped_places))]
  transfers between devices with their start and end apart: 1 -> 0, of which waited for: 1 -> 0; matrix products, arithmetic and copies ran while one was open for 1% -> 0% of each run, Pallas kernels for 0% -> 0%
where the time goes in v1:
time: 111 us
  Pallas kernels  103 us (93%)
  local copies, waits for them, and re-layouts  7.61 us (7%)
    pallas_call x1, Pallas kernels, body(): pl.pallas_call(functools.partial(kernel, groups), out_shape=(out, out), i...  103 us
    unnamed x5, local copies, waits for them, and re-layouts  7.61 us

profile of v1, /device:TPU:1, one launch (start us, length us, event | category | flops | bytes accessed | tf_op | source)
XLA Modules:
  0.0 111.2 jit_solution(13689706594281879578)
XLA Ops:
  0.6 3.4 %copy.6 = s32[64,1,112,32]{3,2,0,1:T(8,128)} copy(s32[64,1,112,32]{2,3,1,0:T(8,128)} %param.6) | data formatting | bytes 1835008 | tf_op args[2]
  4.0 102.9 %shard_map.59 = (f32[64,7168]{1,0:T(8,128)}, f32[64,7168]{1,0:T(8,128)}) custom-call(bf16[64,28672]{1,0:T(8,128)(2,1)} %bitcast.5, f32[64,7168]{1,0:T(8,128)} %bitcast.6, s32[64,14,8,32]{3,2,1,0:T(8,128)} %bitcast.4, bf16[1408,256]{1,0:T(8,128)(2,1)} %constant.2.clone.tab_hbm), custom_call_target="tpu_custom_call" | custom-call | tf_op jit(solution)/shard_map/pallas_call | solution.py:376
  107.0 0.0 copy-start
  107.0 3.0 %copy.9 = f32[1,64,7168]{2,1,0:T(8,128)} copy(f32[1,64,7168]{2,1,0:T(8,128)} %bitcast.7) | data formatting | bytes 3670016
  110.0 0.0 copy-done
  110.0 1.2 %copy.10 = f32[64,7168]{1,0:T(8,128)} copy(f32[64,7168]{1,0:T(8,128)S(1)} %copy-done) | data formatting | bytes 3670016
Async XLA Ops:
  107.0 3.0 %copy-start = (f32[64,7168]{1,0:T(8,128)S(1)}, f32[64,7168]{1,0:T(8,128)}, u32[]{:S(2)}) copy-start(f32[64,7168]{1,0:T(8,128)} %get-tuple-element.9) | copy-start | bytes 5505028

commit v2 on v1

--- a/solution.py
+++ b/solution.py
@@ -19,6 +19,7 @@
 BLOCKS = 8
 WIDTH = BLOCKS * SIDE
 QUAD = 4 * SIDE
+PREP = 2
 DECAY = 0.9
 
 
@@ -78,9 +79,9 @@
 
 
 def kernel(
-    groups, grad_hbm, mom_hbm, idx_hbm, tab_hbm, next_hbm, upd_hbm,
-    grad_v, mom_v, idx_v, tab_v, own_fwd, own_raw, got_fwd, got, next_v, upd_v, y_buf, z_buf, k_buf, l_buf, h_buf, w_buf, s_buf,
-    in_sem, mom_sem, idx_sem, tab_sem, fwd_send, raw_send, sum_send, fwd_recv, got_recv, y_send, y_recv, z_send, z_recv, out_sem,
+    groups, grad_hbm, mom_hbm, idx_hbm, tab_hbm, next_v, upd_v,
+    grad_v, mom_v, idx_v, flat_v, tab_v, own_fwd, own_raw, got_fwd, got, y_buf, z_buf, k_buf, l_buf, h_buf, w_buf, s_buf,
+    in_sem, mom_sem, idx_sem, tab_sem, fwd_send, raw_send, sum_send, fwd_recv, got_recv, y_send, y_recv, z_send, z_recv,
 ):
     width = groups * WIDTH
     half = SIDE // 2
@@ -94,6 +95,9 @@
     def rep_of(z_, place_):
         return z_ * (NY * NC) + place_
 
+    def columns(g):
+        return pl.ds(pl.multiple_of(g * WIDTH, 128), WIDTH)
+
     def load(g, which):
         d = (x + which) % NX
         return pltpu.make_async_copy(
@@ -104,7 +108,7 @@
 
     def load_mom(g):
         return pltpu.make_async_copy(
-            mom_hbm.at[:, pl.ds(pl.multiple_of(g * WIDTH, 128), WIDTH)], mom_v.at[g], mom_sem.at[g]
+            mom_hbm.at[:, columns(g)], mom_v.at[g], mom_sem.at[g]
         )
 
     def start_loads(g):
@@ -185,12 +189,12 @@
         return tab_v[rows[0] : rows[1], :]
 
     def stage_c(g):
-        mine = idx_v[rep, g]
-        spread = jnp.broadcast_to(mine[:, None, :], (BLOCKS, KEEP, KEEP)).reshape(BLOCKS * KEEP, KEEP)
-        row = lax.broadcasted_iota(I32, (BLOCKS * KEEP, KEEP), 0)
-        lane = lax.broadcasted_iota(I32, (BLOCKS * KEEP, KEEP), 1)
-        flat = jnp.sum(jnp.where(row % KEEP == lane, spread, 0), axis=1, keepdims=True)
-        row_of, col_of = flat // SIDE, flat % SIDE
+        mine = flat_v[0, c, pl.ds(pl.multiple_of(g * BLOCKS, BLOCKS), BLOCKS), :]
+        spread = jnp.broadcast_to(mine[:, None, :], (BLOCKS, KEEP, 128)).reshape(BLOCKS * KEEP, 128)
+        slot = lax.broadcasted_iota(I32, (BLOCKS * KEEP, 128), 0) % KEEP + y * KEEP
+        own_lane = lax.broadcasted_iota(I32, (BLOCKS * KEEP, 128), 1) == slot
+        flat = jnp.sum(jnp.where(own_lane, spread, 0), axis=1, keepdims=True)
+        row_of, col_of = flat >> 6, flat & (SIDE - 1)
         row_hot = jnp.where(lax.broadcasted_iota(I32, (BLOCKS * KEEP, SIDE), 1) == row_of, 1.0, 0.0).astype(BF16)
         taken = dot(row_hot, tab(ROWS_LEFT)).astype(BF16)
         block_of = lax.broadcasted_iota(I32, (BLOCKS * KEEP, 1), 0) // KEEP
@@ -202,8 +206,7 @@
         rows_taken = dot(taken, stacked(first))
         kept = jnp.where(hit, rows_taken, 0.0)
         column = jnp.sum(kept, axis=1, keepdims=True)
-        slot = lax.broadcasted_iota(I32, (BLOCKS * KEEP, 128), 0) % KEEP + y * KEEP
-        lanes = jnp.where(lax.broadcasted_iota(I32, (BLOCKS * KEEP, 128), 1) == slot, column, 0.0)
+        lanes = jnp.where(own_lane, column, 0.0)
         y_buf[g, 0] = jnp.sum(lanes.reshape(BLOCKS, KEEP, 128), axis=1)
         for step in range(1, NY * NC):
             copy_y(g, step).start()
@@ -212,13 +215,7 @@
         dims = (((0,), (0,)), ((), ()))
         back = lax.dot_general(both, kh, dims, preferred_element_type=F32)
         back += lax.dot_general(both, kl, dims, preferred_element_type=F32)
-        next_v[g] = acc - right(back[:SIDE] + back[SIDE:], tab(ROWS_INV_H), tab(ROWS_INV_L))
-        write_out(g, next_v, next_hbm, 0).start()
-
-    def write_out(g, src, dst, which):
-        return pltpu.make_async_copy(
-            src.at[g], dst.at[:, pl.ds(pl.multiple_of(g * WIDTH, 128), WIDTH)], out_sem.at[which, g]
-        )
+        next_v[:, columns(g)] = acc - right(back[:SIDE] + back[SIDE:], tab(ROWS_INV_H), tab(ROWS_INV_L))
 
     def stage_d(g):
         drain(y_buf.at[g, pl.ds(1, NY * NC - 1)], y_recv.at[g])
@@ -231,13 +228,17 @@
         for step in range(1, nz):
             copy_z(g, step).start()
 
+    def turn(t):
+        for s in range(PREP):
+            for core in range(NC):
+                other = (z + PREP * t + s) % nz
+                rows = jnp.concatenate([idx_v[rep_of(other, q * NC + core)] for q in range(NY)], axis=0)
+                flat_v[PREP * t + s, core] = jnp.transpose(rows)
+
     def stage_e(g):
-        for t in range(nz):
-            other = (z + t) % nz
-            for core in range(NC):
-                flat = jnp.concatenate([idx_v[rep_of(other, q * NC + core), g] for q in range(NY)], axis=1)
-                k_buf[t, core] = flat // SIDE
-                l_buf[t, core] = flat % SIDE
+        flat = flat_v[:, :, pl.ds(pl.multiple_of(g * BLOCKS, BLOCKS), BLOCKS), :]
+        k_buf[...] = flat >> 6
+        l_buf[...] = flat & (SIDE - 1)
         drain(z_buf.at[g, pl.ds(1, nz - 1)], z_recv.at[g])
         value = z_buf[g]
         high = value.astype(BF16).astype(F32)
@@ -247,21 +248,21 @@
 
         def one_block(j, carry):
             at = pl.ds(j, 1)
-            lhs, rhs_h, rhs_l = [], [], []
+            high_rows, low_rows, cols = [], [], []
             for t in range(nz):
                 for core in range(NC):
                     in_row = level == k_buf[t, core, at, :]
                     in_col = level == l_buf[t, core, at, :]
-                    lhs.append(jnp.where(in_row, 1.0, 0.0).astype(BF16))
-                    rhs_h.append(jnp.where(in_col, h_buf[t, core, at, :], 0.0).astype(BF16))
-                    rhs_l.append(jnp.where(in_col, w_buf[t, core, at, :], 0.0).astype(BF16))
-            a = jnp.concatenate(lhs, axis=1)
-            b = jnp.concatenate([jnp.concatenate(rhs_h, axis=1), jnp.concatenate(rhs_l, axis=1)], axis=0)
+                    high_rows.append(jnp.where(in_row, h_buf[t, core, at, :], 0.0).astype(BF16))
+                    low_rows.append(jnp.where(in_row, w_buf[t, core, at, :], 0.0).astype(BF16))
+                    cols.append(jnp.where(in_col, 1.0, 0.0).astype(BF16))
+            a = jnp.concatenate([jnp.concatenate(high_rows, axis=1), jnp.concatenate(low_rows, axis=1)], axis=0)
+            b = jnp.concatenate(cols, axis=1)
             s_buf[j] = lax.dot_general(a, b, (((1,), (1,)), ((), ())), preferred_element_type=F32)
             return carry
 
-        lax.fori_loop(0, BLOCKS, one_block, 0)
-        total = jnp.concatenate([s_buf[j, :, :SIDE] + s_buf[j, :, SIDE:] for j in range(BLOCKS)], axis=1)
+        lax.fori_loop(0, BLOCKS, one_block, 0, unroll=BLOCKS)
+        total = jnp.concatenate([s_buf[j, :SIDE] + s_buf[j, SIDE:] for j in range(BLOCKS)], axis=1)
         total = total * (1.0 / (nz * NY * NC))
         first = dot(tab(ROWS_LEFT_T), stacked(total))
         decoded = right(first, tab(ROWS_INV_H), tab(ROWS_INV_L))
@@ -269,8 +270,7 @@
         sh, sl = two(jnp.concatenate([squares[:, :QUAD], squares[:, QUAD:]] + [jnp.zeros((6, QUAD), F32)], axis=0))
         q = dot(sh, tab(ROWS_ONES)) + dot(sl, tab(ROWS_ONES))
         scale = 1.0 / jnp.sqrt(q * (1.0 / (SIDE * SIDE)) + 1e-6)
-        upd_v[g] = decoded * jnp.concatenate([scale[0:1], scale[1:2]], axis=1)
-        write_out(g, upd_v, upd_hbm, 1).start()
+        upd_v[:, columns(g)] = decoded * jnp.concatenate([scale[0:1], scale[1:2]], axis=1)
 
     start_loads(0)
     barrier = pltpu.get_barrier_semaphore()
@@ -302,30 +302,30 @@
         at(0, stage_a)
         at(1, stage_b)
 
-        @pl.when(t == 2)
+        @pl.when(t == 0)
+        def _():
+            load_idx.wait()
+
+        @pl.when(t == 1)
         def _():
             load_tab.wait()
-            load_idx.wait()
-
+
+        @pl.when(t < nz // PREP)
+        def _():
+            turn(t)
+
+        at(5, stage_e)
         at(2, stage_c)
         at(3, stage_d)
-        at(4, stage_e)
         return carry
 
-    lax.fori_loop(0, groups + 4, step, 0)
+    lax.fori_loop(0, groups + 5, step, 0)
 
     drain(own_fwd.at[pl.ds(0, groups)], fwd_send)
     drain(own_fwd.at[pl.ds(groups, groups)], sum_send)
     drain(own_raw, raw_send)
     drain(y_buf.at[:, pl.ds(1, NY * NC - 1)], y_send)
     drain(z_buf.at[:, pl.ds(1, nz - 1)], z_send)
-
-    def finish(g, carry):
-        write_out(g, next_v, next_hbm, 0).wait()
-        write_out(g, upd_v, upd_hbm, 1).wait()
-        return carry
-
-    lax.fori_loop(0, groups, finish, 0)
 
 
 def body(grad_parts, momentum, indices):
@@ -335,28 +335,27 @@
     groups = width // WIDTH
     reps = indices.shape[0]
     nz = reps // (NY * NC)
-    idx = indices.reshape(reps, groups, BLOCKS, KEEP)
+    idx = jnp.transpose(indices[:, 0], (0, 2, 1))
     half = SIDE // 2
     dma = pltpu.SemaphoreType.DMA
     any_space = pl.BlockSpec(memory_space=pl.ANY)
     scratch = [
         pltpu.VMEM((NX, groups, SIDE, WIDTH), BF16),
         pltpu.VMEM((groups, SIDE, WIDTH), F32),
-        pltpu.VMEM((reps, groups, BLOCKS, KEEP), I32),
+        pltpu.VMEM((reps, KEEP, groups * BLOCKS), I32),
+        pltpu.VMEM((nz, NC, groups * BLOCKS, 128), I32),
         pltpu.VMEM((1408, QUAD), BF16),
         pltpu.VMEM((2 * groups, 2, half, WIDTH), F32),
         pltpu.VMEM((groups, 2, half, WIDTH), F32),
         pltpu.VMEM((groups, 2, half, WIDTH), F32),
         pltpu.VMEM((groups, 2, SIDE, WIDTH), F32),
-        pltpu.VMEM((groups, SIDE, WIDTH), F32),
-        pltpu.VMEM((groups, SIDE, WIDTH), F32),
         pltpu.VMEM((groups, NY * NC, BLOCKS, 128), F32),
         pltpu.VMEM((groups, nz, NC, BLOCKS, 128), F32),
         pltpu.VMEM((nz, NC, BLOCKS, 128), I32),
         pltpu.VMEM((nz, NC, BLOCKS, 128), I32),
         pltpu.VMEM((nz, NC, BLOCKS, 128), F32),
         pltpu.VMEM((nz, NC, BLOCKS, 128), F32),
-        pltpu.VMEM((BLOCKS, SIDE, 2 * SIDE), F32),
+        pltpu.VMEM((BLOCKS, 2 * SIDE, SIDE), F32),
         dma((NX, groups)),
         dma((groups,)),
         dma,
@@ -370,14 +369,13 @@
         dma((groups,)),
         dma,
         dma((groups,)),
-        dma((2, groups)),
     ]
-    out = jax.ShapeDtypeStruct((rows, width), F32)
+    out = pltpu.VMEM((rows, width), F32)
     moment_next, update = pl.pallas_call(
         functools.partial(kernel, groups),
         out_shape=(out, out),
         in_specs=[any_space] * 4,
-        out_specs=(any_space, any_space),
+        out_specs=(pl.BlockSpec(memory_space=pltpu.VMEM),) * 2,
         scratch_shapes=scratch,
         compiler_params=pltpu.CompilerParams(
             collective_id=0, has_side_effects=True, vmem_limit_bytes=56 * 1024 * 1024

time: 111 us -> 90.4 us (0.81)
  Pallas kernels: 103 us -> 87.2 us
  local copies, waits for them, and re-layouts: 7.61 us -> 2.46 us
    pallas_call x1, Pallas kernels: 103 us -> 87.2 us  [body(): pl.pallas_call(functools.partial(kernel, groups), out_shape=(out, out), i...]
    unnamed x5 -> x2, local copies, waits for them, and re-layouts: 7.61 us -> 2.46 us
where the time goes in v2:
time: 90.4 us; the launch traced here: 90.3 us
  Pallas kernels  87.2 us (96%)
  local copies, waits for them, and re-layouts  2.46 us (3%)
    pallas_call x1, Pallas kernels, body(): pl.pallas_call(functools.partial(kernel, groups), out_shape=(out, out), i...  87.2 us
    unnamed x2, local copies, waits for them, and re-layouts  2.46 us

profile of v2, /device:TPU:1, one launch (start us, length us, event | category | flops | bytes accessed | tf_op | source)
XLA Modules:
  0.0 90.3 jit_solution(11855259371270943606)
XLA Ops:
  0.6 87.2 %shard_map.59 = (f32[64,7168]{1,0:T(8,128)S(1)}, f32[64,7168]{1,0:T(8,128)S(1)}) custom-call(bf16[64,28672]{1,0:T(8,128)(2,1)} %bitcast.7, f32[64,7168]{1,0:T(8,128)} %bitcast.8, s32[64,32,112]{2,1,0:T(8,128)} %bitcast.9, bf16[1408,256]{1,0:T(8,128)(2,1)} %constant.2.clone.tab_hbm), custom_call_target="tpu_custom_call" | custom-call | tf_op jit(solution)/shard_map/pallas_call | solution.py:374
  87.8 1.2 %copy.8 = f32[1,64,7168]{2,1,0:T(8,128)} copy(f32[1,64,7168]{2,1,0:T(8,128)S(1)} %bitcast.6) | data formatting | bytes 3670016
  89.0 1.2 %copy.9 = f32[64,7168]{1,0:T(8,128)} copy(f32[64,7168]{1,0:T(8,128)S(1)} %get-tuple-element.7) | data formatting | bytes 3670016

commit v3 on v2

--- a/solution.py
+++ b/solution.py
@@ -20,6 +20,11 @@
 WIDTH = BLOCKS * SIDE
 QUAD = 4 * SIDE
 PREP = 2
+EARLY = 3
+HALF = BLOCKS // 2
+PICK_AT = 2
+SUM_AT = 11
+LAG_E = 5
 DECAY = 0.9
 
 
@@ -66,11 +71,13 @@
 
 def right(x, high, low):
     xh, xl = two(x)
-    stack = jnp.concatenate([xh[:, :QUAD], xh[:, QUAD:], xl[:, :QUAD], xl[:, QUAD:]], axis=0)
+    quads = range(x.shape[1] // QUAD)
+    rows = len(quads) * SIDE
+    parts = [v[:, q * QUAD : (q + 1) * QUAD] for v in (xh, xl) for q in quads]
+    stack = jnp.concatenate(parts, axis=0)
     p = dot(stack, high)
-    q = dot(stack[: 2 * SIDE], low)
-    s = p[: 2 * SIDE] + p[2 * SIDE :] + q
-    return jnp.concatenate([s[:SIDE], s[SIDE:]], axis=1)
+    s = p[:rows] + p[rows:] + dot(stack[:rows], low)
+    return jnp.concatenate([s[q * SIDE : (q + 1) * SIDE] for q in quads], axis=1)
 
 
 def stacked(y):
@@ -80,8 +87,8 @@
 
 def kernel(
     groups, grad_hbm, mom_hbm, idx_hbm, tab_hbm, next_v, upd_v,
-    grad_v, mom_v, idx_v, flat_v, tab_v, own_fwd, own_raw, got_fwd, got, y_buf, z_buf, k_buf, l_buf, h_buf, w_buf, s_buf,
-    in_sem, mom_sem, idx_sem, tab_sem, fwd_send, raw_send, sum_send, fwd_recv, got_recv, y_send, y_recv, z_send, z_recv,
+    grad_v, mom_v, idx_v, flat_v, tab_v, own_fwd, own_raw, got_fwd, got, xi_buf, p_own, p_got, y_buf, z_buf, k_buf, l_buf, h_buf, w_buf, s_buf,
+    in_sem, mom_sem, idx_sem, tab_sem, fwd_send, raw_send, sum_send, fwd_recv, got_recv, xi_send, xi_recv, p_send, p_recv, u_send, u_recv, y_send, y_recv, z_send, z_recv,
 ):
     width = groups * WIDTH
     half = SIDE // 2
@@ -91,6 +98,7 @@
     z, y, c = rep // (NY * NC), (rep // NC) % NY, rep % NC
     left, right_x, far = (x + NX - 1) % NX, (x + 1) % NX, (x + 2) % NX
     place = y * NC + c
+    first_early = groups - EARLY
 
     def rep_of(z_, place_):
         return z_ * (NY * NC) + place_
@@ -140,6 +148,26 @@
         return to_x(
             own_fwd.at[groups + g, way], got.at[g, way, rows], sum_send, got_recv.at[g], left if way == 0 else right_x
         )
+
+    def copy_xi(s):
+        return to_x(xi_buf.at[0], xi_buf.at[NX - s], xi_send, xi_recv, (x + s) % NX)
+
+    def copy_p(e, s):
+        return to_x(p_own.at[e, s - 1], p_got.at[e, NX - s], p_send, p_recv.at[e], (x + s) % NX)
+
+    def copy_u(g):
+        half_of = upd_v.at[:, half_columns(g)]
+        return pltpu.make_async_remote_copy(
+            src_ref=half_of,
+            dst_ref=half_of,
+            send_sem=u_send,
+            recv_sem=u_recv,
+            device_id=(rep + 1 - 2 * c, x),
+            device_id_type=MESH,
+        )
+
+    def half_columns(g):
+        return pl.ds(pl.multiple_of(g * WIDTH + c * (WIDTH // NC), 128), WIDTH // NC)
 
     def copy_y(g, step):
         other = (place + step) % (NY * NC)
@@ -166,9 +194,16 @@
     def drain(ref, sem):
         pltpu.make_async_copy(ref, ref, sem).wait()
 
-    def stage_a(g):
+    def wait_loads(g):
         for which in (2, 3, 1, 0):
             load(g, which).wait()
+        load_mom(g).wait()
+
+    def stage_a(g):
+        @pl.when(g < first_early)
+        def _():
+            wait_loads(g)
+
         own_fwd[g, 0] = grad_v[2, g, :half].astype(F32)
         copy_fwd(g, 0).start()
         own_fwd[g, 1] = grad_v[2, g, half:].astype(F32)
@@ -188,34 +223,94 @@
     def tab(rows):
         return tab_v[rows[0] : rows[1], :]
 
-    def stage_c(g):
-        mine = flat_v[0, c, pl.ds(pl.multiple_of(g * BLOCKS, BLOCKS), BLOCKS), :]
-        spread = jnp.broadcast_to(mine[:, None, :], (BLOCKS, KEEP, 128)).reshape(BLOCKS * KEEP, 128)
+    def own_lanes():
         slot = lax.broadcasted_iota(I32, (BLOCKS * KEEP, 128), 0) % KEEP + y * KEEP
-        own_lane = lax.broadcasted_iota(I32, (BLOCKS * KEEP, 128), 1) == slot
-        flat = jnp.sum(jnp.where(own_lane, spread, 0), axis=1, keepdims=True)
+        return lax.broadcasted_iota(I32, (BLOCKS * KEEP, 128), 1) == slot
+
+    def as_column(rows, zero):
+        spread = jnp.broadcast_to(rows[:, None, :], (BLOCKS, KEEP, 128)).reshape(BLOCKS * KEEP, 128)
+        return jnp.sum(jnp.where(own_lanes(), spread, zero), axis=1, keepdims=True)
+
+    def as_rows(column):
+        lanes = jnp.where(own_lanes(), column, 0.0)
+        return jnp.sum(lanes.reshape(BLOCKS, KEEP, 128), axis=1)
+
+    def places(rows):
+        flat = as_column(rows, 0)
         row_of, col_of = flat >> 6, flat & (SIDE - 1)
         row_hot = jnp.where(lax.broadcasted_iota(I32, (BLOCKS * KEEP, SIDE), 1) == row_of, 1.0, 0.0).astype(BF16)
         taken = dot(row_hot, tab(ROWS_LEFT)).astype(BF16)
         block_of = lax.broadcasted_iota(I32, (BLOCKS * KEEP, 1), 0) // KEEP
         hit = lax.broadcasted_iota(I32, (BLOCKS * KEEP, WIDTH), 1) == block_of * SIDE + col_of
-        drain(got.at[g], got_recv.at[g])
-        load_mom(g).wait()
-        acc = DECAY * mom_v[g] + (grad_v[0, g].astype(F32) + (got[g, 0] + got[g, 1]))
-        first = right(acc, tab(ROWS_FWD_H), tab(ROWS_FWD_L))
-        rows_taken = dot(taken, stacked(first))
-        kept = jnp.where(hit, rows_taken, 0.0)
-        column = jnp.sum(kept, axis=1, keepdims=True)
-        lanes = jnp.where(own_lane, column, 0.0)
-        y_buf[g, 0] = jnp.sum(lanes.reshape(BLOCKS, KEEP, 128), axis=1)
-        for step in range(1, NY * NC):
-            copy_y(g, step).start()
+        return taken, hit
+
+    def pick(field, taken, hit):
+        first = right(field, tab(ROWS_FWD_H), tab(ROWS_FWD_L))
+        kept = jnp.where(hit, dot(taken, stacked(first)), 0.0)
+        return kept, jnp.sum(kept, axis=1, keepdims=True)
+
+    def put_back(kept, taken):
         kh, kl = two(kept)
         both = taken[:, : 2 * SIDE]
         dims = (((0,), (0,)), ((), ()))
         back = lax.dot_general(both, kh, dims, preferred_element_type=F32)
         back += lax.dot_general(both, kl, dims, preferred_element_type=F32)
-        next_v[:, columns(g)] = acc - right(back[:SIDE] + back[SIDE:], tab(ROWS_INV_H), tab(ROWS_INV_L))
+        return right(back[:SIDE] + back[SIDE:], tab(ROWS_INV_H), tab(ROWS_INV_L))
+
+    def own_rows(g):
+        return flat_v[0, c, pl.ds(pl.multiple_of(g * BLOCKS, BLOCKS), BLOCKS), :]
+
+    def summed(g):
+        drain(got.at[g], got_recv.at[g])
+        return DECAY * mom_v[g] + (grad_v[0, g].astype(F32) + (got[g, 0] + got[g, 1]))
+
+    def send_y(g):
+        for step in range(1, NY * NC):
+            copy_y(g, step).start()
+
+    def stage_c(g):
+        taken, hit = places(own_rows(g))
+        acc = summed(g)
+        kept, column = pick(acc, taken, hit)
+        y_buf[g, 0] = as_rows(column)
+        send_y(g)
+        next_v[:, columns(g)] = acc - put_back(kept, taken)
+
+    def early_pick(e):
+        g = first_early + e
+        wait_loads(g)
+
+        def one_shard(s, carry):
+            rows = xi_buf[s, pl.ds(pl.multiple_of(e * BLOCKS, BLOCKS), BLOCKS), :]
+            taken, hit = places(rows)
+            field = grad_v[s, g].astype(F32) + jnp.where(s == 0, DECAY, 0.0) * mom_v[g]
+            picked = as_rows(pick(field, taken, hit)[1])
+
+            @pl.when(s == 0)
+            def _():
+                p_got[e, 0] = picked
+
+            @pl.when(s > 0)
+            def _():
+                p_own[e, s - 1] = picked
+                copy_p(e, s).start()
+
+            return carry
+
+        lax.fori_loop(0, NX, one_shard, 0)
+
+    def early_sum(e):
+        g = first_early + e
+        taken, hit = places(own_rows(g))
+        drain(p_got.at[e, pl.ds(1, NX - 1)], p_recv.at[e])
+        rows = (p_got[e, 0] + p_got[e, 1]) + (p_got[e, 2] + p_got[e, 3])
+        y_buf[g, 0] = rows
+        send_y(g)
+        kept = jnp.where(hit, as_column(rows, 0.0), 0.0)
+        next_v[:, columns(g)] = put_back(kept, taken)
+
+    def early_end(g):
+        next_v[:, columns(g)] = summed(g) - next_v[:, columns(g)]
 
     def stage_d(g):
         drain(y_buf.at[g, pl.ds(1, NY * NC - 1)], y_recv.at[g])
@@ -235,12 +330,15 @@
                 rows = jnp.concatenate([idx_v[rep_of(other, q * NC + core)] for q in range(NY)], axis=0)
                 flat_v[PREP * t + s, core] = jnp.transpose(rows)
 
+    def own_half(rows):
+        return jnp.where(c == 0, rows[:, :, :HALF], rows[:, :, HALF:])
+
     def stage_e(g):
-        flat = flat_v[:, :, pl.ds(pl.multiple_of(g * BLOCKS, BLOCKS), BLOCKS), :]
+        flat = own_half(flat_v[:, :, pl.ds(pl.multiple_of(g * BLOCKS, BLOCKS), BLOCKS), :])
         k_buf[...] = flat >> 6
         l_buf[...] = flat & (SIDE - 1)
         drain(z_buf.at[g, pl.ds(1, nz - 1)], z_recv.at[g])
-        value = z_buf[g]
+        value = own_half(z_buf[g])
         high = value.astype(BF16).astype(F32)
         h_buf[...] = high
         w_buf[...] = value - high
@@ -261,20 +359,20 @@
             s_buf[j] = lax.dot_general(a, b, (((1,), (1,)), ((), ())), preferred_element_type=F32)
             return carry
 
-        lax.fori_loop(0, BLOCKS, one_block, 0, unroll=BLOCKS)
-        total = jnp.concatenate([s_buf[j, :SIDE] + s_buf[j, SIDE:] for j in range(BLOCKS)], axis=1)
+        lax.fori_loop(0, HALF, one_block, 0, unroll=HALF)
+        total = jnp.concatenate([s_buf[j, :SIDE] + s_buf[j, SIDE:] for j in range(HALF)], axis=1)
         total = total * (1.0 / (nz * NY * NC))
         first = dot(tab(ROWS_LEFT_T), stacked(total))
         decoded = right(first, tab(ROWS_INV_H), tab(ROWS_INV_L))
         squares = jnp.sum(decoded * decoded, axis=0, keepdims=True)
-        sh, sl = two(jnp.concatenate([squares[:, :QUAD], squares[:, QUAD:]] + [jnp.zeros((6, QUAD), F32)], axis=0))
+        sh, sl = two(jnp.broadcast_to(squares, (8, QUAD)))
         q = dot(sh, tab(ROWS_ONES)) + dot(sl, tab(ROWS_ONES))
-        scale = 1.0 / jnp.sqrt(q * (1.0 / (SIDE * SIDE)) + 1e-6)
-        upd_v[:, columns(g)] = decoded * jnp.concatenate([scale[0:1], scale[1:2]], axis=1)
+        upd_v[:, half_columns(g)] = decoded * (1.0 / jnp.sqrt(q[0:1] * (1.0 / (SIDE * SIDE)) + 1e-6))
+        copy_u(g).start()
 
     start_loads(0)
     barrier = pltpu.get_barrier_semaphore()
-    for where in (left, right_x):
+    for where in (left, right_x, far):
         pl.semaphore_signal(barrier, inc=1, device_id=(rep, where), device_id_type=MESH)
     for step in range(1, NY * NC):
         pl.semaphore_signal(
@@ -283,47 +381,76 @@
     for step in range(1, nz):
         pl.semaphore_signal(barrier, inc=1, device_id=(rep_of((z + step) % nz, place), x), device_id_type=MESH)
     start_loads(1)
+    load_idx.start()
     load_tab.start()
-    load_idx.start()
-    pl.semaphore_wait(barrier, 2 + NY * NC - 1 + nz - 1)
+    for e in range(EARLY):
+        start_loads(first_early + e)
+    pl.semaphore_wait(barrier, NX - 1 + NY * NC - 1 + nz - 1)
 
     def step(t, carry):
-        def at(lag, stage):
-            g = t - lag
-
-            @pl.when((g >= 0) & (g < groups))
+        def at(first, count, stage):
+            @pl.when((t >= first) & (t < first + count))
             def _():
-                stage(g)
-
-        @pl.when(t + 2 < groups)
+                stage(t - first)
+
+        def both(stage, lag, early_at):
+            def one(k, carry):
+                g = jnp.where(k == 0, t - lag, first_early + t - early_at)
+                due = jnp.where(k == 0, (g >= 0) & (g < first_early), (g >= first_early) & (g < groups))
+
+                @pl.when(due)
+                def _():
+                    stage(g)
+
+                return carry
+
+            lax.fori_loop(0, 2, one, 0)
+
+        @pl.when(t + 2 < first_early)
         def _():
             start_loads(t + 2)
 
-        at(0, stage_a)
-        at(1, stage_b)
+        at(0, groups, stage_a)
+        at(1, groups, stage_b)
 
         @pl.when(t == 0)
         def _():
             load_idx.wait()
 
+        at(0, nz // PREP, turn)
+
+        @pl.when(t == 0)
+        def _():
+            xi_buf[0] = flat_v[0, c, first_early * BLOCKS :, :]
+            for s in range(1, NX):
+                copy_xi(s).start()
+
         @pl.when(t == 1)
         def _():
             load_tab.wait()
 
-        @pl.when(t < nz // PREP)
+        both(stage_e, LAG_E, SUM_AT)
+
+        @pl.when(t == PICK_AT)
         def _():
-            turn(t)
-
-        at(5, stage_e)
-        at(2, stage_c)
-        at(3, stage_d)
+            drain(xi_buf.at[pl.ds(1, NX - 1)], xi_recv)
+
+        at(PICK_AT, EARLY, early_pick)
+        at(PICK_AT + 2, EARLY, early_sum)
+        at(2, first_early, stage_c)
+        at(2 + first_early, EARLY, lambda e: early_end(first_early + e))
+        both(stage_d, 3, PICK_AT + 3)
         return carry
 
-    lax.fori_loop(0, groups + 5, step, 0)
+    lax.fori_loop(0, max(groups + 2, first_early + LAG_E, SUM_AT + EARLY), step, 0)
 
     drain(own_fwd.at[pl.ds(0, groups)], fwd_send)
     drain(own_fwd.at[pl.ds(groups, groups)], sum_send)
     drain(own_raw, raw_send)
+    drain(xi_buf.at[pl.ds(1, NX - 1)], xi_send)
+    drain(p_own, p_send)
+    drain(upd_v.at[:, : width // NC], u_send)
+    drain(upd_v.at[:, : width // NC], u_recv)
     drain(y_buf.at[:, pl.ds(1, NY * NC - 1)], y_send)
     drain(z_buf.at[:, pl.ds(1, nz - 1)], z_send)
 
@@ -349,13 +476,16 @@
         pltpu.VMEM((groups, 2, half, WIDTH), F32),
         pltpu.VMEM((groups, 2, half, WIDTH), F32),
         pltpu.VMEM((groups, 2, SIDE, WIDTH), F32),
+        pltpu.VMEM((NX, EARLY * BLOCKS, 128), I32),
+        pltpu.VMEM((EARLY, NX - 1, BLOCKS, 128), F32),
+        pltpu.VMEM((EARLY, NX, BLOCKS, 128), F32),
         pltpu.VMEM((groups, NY * NC, BLOCKS, 128), F32),
         pltpu.VMEM((groups, nz, NC, BLOCKS, 128), F32),
-        pltpu.VMEM((nz, NC, BLOCKS, 128), I32),
-        pltpu.VMEM((nz, NC, BLOCKS, 128), I32),
-        pltpu.VMEM((nz, NC, BLOCKS, 128), F32),
-        pltpu.VMEM((nz, NC, BLOCKS, 128), F32),
-        pltpu.VMEM((BLOCKS, 2 * SIDE, SIDE), F32),
+        pltpu.VMEM((nz, NC, HALF, 128), I32),
+        pltpu.VMEM((nz, NC, HALF, 128), I32),
+        pltpu.VMEM((nz, NC, HALF, 128), F32),
+        pltpu.VMEM((nz, NC, HALF, 128), F32),
+        pltpu.VMEM((HALF, 2 * SIDE, SIDE), F32),
         dma((NX, groups)),
         dma((groups,)),
         dma,
@@ -365,6 +495,12 @@
         dma,
         dma((groups,)),
         dma((groups,)),
+        dma,
+        dma,
+        dma,
+        dma((EARLY,)),
+        dma,
+        dma,
         dma,
         dma((groups,)),
         dma,

time: 90.4 us -> 80.9 us (0.89)
  Pallas kernels: 87.2 us -> 77.7 us
    pallas_call x1, Pallas kernels: 87.2 us -> 77.7 us  [body(): pl.pallas_call(functools.partial(kernel, groups), out_shape=(out, out), i...]
where the time goes in v3:
time: 80.9 us; the launch traced here: 80.8 us
  Pallas kernels  77.7 us (96%)
  local copies, waits for them, and re-layouts  2.46 us (3%)
    pallas_call x1, Pallas kernels, body(): pl.pallas_call(functools.partial(kernel, groups), out_shape=(out, out), i...  77.7 us
    unnamed x2, local copies, waits for them, and re-layouts  2.46 us

profile of v3, /device:TPU:1, one launch (start us, length us, event | category | flops | bytes accessed | tf_op | source)
XLA Modules:
  0.0 80.8 jit_solution(2544213550763381925)
XLA Ops:
  0.6 77.7 %shard_map.59 = (f32[64,7168]{1,0:T(8,128)S(1)}, f32[64,7168]{1,0:T(8,128)S(1)}) custom-call(bf16[64,28672]{1,0:T(8,128)(2,1)} %bitcast.7, f32[64,7168]{1,0:T(8,128)} %bitcast.8, s32[64,32,112]{2,1,0:T(8,128)} %bitcast.9, bf16[1408,256]{1,0:T(8,128)(2,1)} %constant.2.clone.tab_hbm), custom_call_target="tpu_custom_call" | custom-call | tf_op jit(solution)/shard_map/pallas_call | solution.py:510
  78.3 1.2 %copy.8 = f32[1,64,7168]{2,1,0:T(8,128)} copy(f32[1,64,7168]{2,1,0:T(8,128)S(1)} %bitcast.6) | data formatting | bytes 3670016
  79.5 1.2 %copy.9 = f32[64,7168]{1,0:T(8,128)} copy(f32[64,7168]{1,0:T(8,128)S(1)} %get-tuple-element.7) | data formatting | bytes 3670016

commit v4 on v3

--- a/solution.py
+++ b/solution.py
@@ -20,11 +20,12 @@
 WIDTH = BLOCKS * SIDE
 QUAD = 4 * SIDE
 PREP = 2
-EARLY = 3
+PARTS = 1
+EARLY = 5
 HALF = BLOCKS // 2
-PICK_AT = 2
-SUM_AT = 11
-LAG_E = 5
+PICK_AT = 1
+SUM_AT = 10
+LAG_E = 6
 DECAY = 0.9
 
 
@@ -80,6 +81,13 @@
     return jnp.concatenate([s[q * SIDE : (q + 1) * SIDE] for q in quads], axis=1)
 
 
+def right_exact(x, high, low):
+    quads = range(x.shape[1] // QUAD)
+    stack = jnp.concatenate([x[:, q * QUAD : (q + 1) * QUAD] for q in quads], axis=0)
+    s = dot(stack, high) + dot(stack, low)
+    return jnp.concatenate([s[q * SIDE : (q + 1) * SIDE] for q in quads], axis=1)
+
+
 def stacked(y):
     yh, yl = two(y)
     return jnp.concatenate([yh, yh, yl, yl], axis=0)
@@ -88,7 +96,7 @@
 def kernel(
     groups, grad_hbm, mom_hbm, idx_hbm, tab_hbm, next_v, upd_v,
     grad_v, mom_v, idx_v, flat_v, tab_v, own_fwd, own_raw, got_fwd, got, xi_buf, p_own, p_got, y_buf, z_buf, k_buf, l_buf, h_buf, w_buf, s_buf,
-    in_sem, mom_sem, idx_sem, tab_sem, fwd_send, raw_send, sum_send, fwd_recv, got_recv, xi_send, xi_recv, p_send, p_recv, u_send, u_recv, y_send, y_recv, z_send, z_recv,
+    in_sem, mom_sem, idx_sem, tab_sem, fwd_send, raw_send, sum_send, fwd_recv, got_recv, xi_send, xi_recv, p_send, p_recv, u_send, u_recv, y_send, y_recv, z_send, z_recv, here_sem,
 ):
     width = groups * WIDTH
     half = SIDE // 2
@@ -199,19 +207,25 @@
             load(g, which).wait()
         load_mom(g).wait()
 
+    def widen(g):
+        own_fwd[g, 0] = grad_v[2, g, :half].astype(F32)
+        own_fwd[g, 1] = grad_v[2, g, half:].astype(F32)
+        own_raw[g, 0] = grad_v[3, g, half:].astype(F32)
+        own_raw[g, 1] = grad_v[1, g, :half].astype(F32)
+
+    def send_a(g):
+        copy_fwd(g, 0).start()
+        copy_fwd(g, 1).start()
+        copy_raw(g, 0).start()
+        copy_raw(g, 1).start()
+
     def stage_a(g):
         @pl.when(g < first_early)
         def _():
             wait_loads(g)
 
-        own_fwd[g, 0] = grad_v[2, g, :half].astype(F32)
-        copy_fwd(g, 0).start()
-        own_fwd[g, 1] = grad_v[2, g, half:].astype(F32)
-        copy_fwd(g, 1).start()
-        own_raw[g, 0] = grad_v[3, g, half:].astype(F32)
-        copy_raw(g, 0).start()
-        own_raw[g, 1] = grad_v[1, g, :half].astype(F32)
-        copy_raw(g, 1).start()
+        widen(g)
+        send_a(g)
 
     def stage_b(g):
         drain(got_fwd.at[g], fwd_recv.at[g])
@@ -245,7 +259,7 @@
         return taken, hit
 
     def pick(field, taken, hit):
-        first = right(field, tab(ROWS_FWD_H), tab(ROWS_FWD_L))
+        first = (right_exact if field.dtype == BF16 else right)(field, tab(ROWS_FWD_H), tab(ROWS_FWD_L))
         kept = jnp.where(hit, dot(taken, stacked(first)), 0.0)
         return kept, jnp.sum(kept, axis=1, keepdims=True)
 
@@ -260,8 +274,10 @@
     def own_rows(g):
         return flat_v[0, c, pl.ds(pl.multiple_of(g * BLOCKS, BLOCKS), BLOCKS), :]
 
+    def wait_sums(g):
+        drain(got.at[g], got_recv.at[g])
+
     def summed(g):
-        drain(got.at[g], got_recv.at[g])
         return DECAY * mom_v[g] + (grad_v[0, g].astype(F32) + (got[g, 0] + got[g, 1]))
 
     def send_y(g):
@@ -276,28 +292,23 @@
         send_y(g)
         next_v[:, columns(g)] = acc - put_back(kept, taken)
 
-    def early_pick(e):
+    def early_own(e, carry):
         g = first_early + e
         wait_loads(g)
-
+        taken, hit = places(own_rows(g))
+        field = grad_v[0, g].astype(F32) + DECAY * mom_v[g]
+        p_got[e, 0] = as_rows(pick(field, taken, hit)[1])
+        return carry
+
+    def early_pick(e):
         def one_shard(s, carry):
             rows = xi_buf[s, pl.ds(pl.multiple_of(e * BLOCKS, BLOCKS), BLOCKS), :]
             taken, hit = places(rows)
-            field = grad_v[s, g].astype(F32) + jnp.where(s == 0, DECAY, 0.0) * mom_v[g]
-            picked = as_rows(pick(field, taken, hit)[1])
-
-            @pl.when(s == 0)
-            def _():
-                p_got[e, 0] = picked
-
-            @pl.when(s > 0)
-            def _():
-                p_own[e, s - 1] = picked
-                copy_p(e, s).start()
-
+            p_own[e, s - 1] = as_rows(pick(grad_v[s, first_early + e], taken, hit)[1])
+            copy_p(e, s).start()
             return carry
 
-        lax.fori_loop(0, NX, one_shard, 0)
+        lax.fori_loop(1, NX, one_shard, 0, unroll=NX - 1)
 
     def early_sum(e):
         g = first_early + e
@@ -370,22 +381,47 @@
         upd_v[:, half_columns(g)] = decoded * (1.0 / jnp.sqrt(q[0:1] * (1.0 / (SIDE * SIDE)) + 1e-6))
         copy_u(g).start()
 
-    start_loads(0)
     barrier = pltpu.get_barrier_semaphore()
-    for where in (left, right_x, far):
-        pl.semaphore_signal(barrier, inc=1, device_id=(rep, where), device_id_type=MESH)
+    for step in (1, nz - 1):
+        pl.semaphore_signal(barrier, inc=1, device_id=(rep_of((z + step) % nz, place), x), device_id_type=MESH)
     for step in range(1, NY * NC):
         pl.semaphore_signal(
             barrier, inc=1, device_id=(rep_of(z, (place + step) % (NY * NC)), x), device_id_type=MESH
         )
-    for step in range(1, nz):
-        pl.semaphore_signal(barrier, inc=1, device_id=(rep_of((z + step) % nz, place), x), device_id_type=MESH)
-    start_loads(1)
+    for where in (far, left, right_x):
+        pl.semaphore_signal(barrier, inc=1, device_id=(rep, where), device_id_type=MESH)
     load_idx.start()
     load_tab.start()
+    start_loads(0)
     for e in range(EARLY):
         start_loads(first_early + e)
-    pl.semaphore_wait(barrier, NX - 1 + NY * NC - 1 + nz - 1)
+    start_loads(1)
+    load_idx.wait()
+
+    def turn_part(t, carry):
+        turn(t)
+        return carry
+
+    lax.fori_loop(0, nz // PREP, turn_part, 0)
+    xi_buf[0] = flat_v[0, c, first_early * BLOCKS :, :]
+    wait_loads(0)
+    widen(0)
+    load_tab.wait()
+    pl.semaphore_wait(barrier, NX - 1 + NY * NC - 1 + 2)
+    send_a(0)
+    for s in range(1, NX):
+        copy_xi(s).start()
+    stage_a(1)
+    lax.fori_loop(0, EARLY, early_own, 0)
+
+    def greet(t):
+        for way in (1, nz - 1):
+            pl.semaphore_signal(
+                here_sem.at[t], inc=1, device_id=(rep_of((z + way) % nz, place), x), device_id_type=MESH
+            )
+
+    def met(t):
+        pl.semaphore_wait(here_sem.at[t], 2)
 
     def step(t, carry):
         def at(first, count, stage):
@@ -410,25 +446,11 @@
         def _():
             start_loads(t + 2)
 
-        at(0, groups, stage_a)
         at(1, groups, stage_b)
 
-        @pl.when(t == 0)
-        def _():
-            load_idx.wait()
-
-        at(0, nz // PREP, turn)
-
-        @pl.when(t == 0)
-        def _():
-            xi_buf[0] = flat_v[0, c, first_early * BLOCKS :, :]
-            for s in range(1, NX):
-                copy_xi(s).start()
-
-        @pl.when(t == 1)
-        def _():
-            load_tab.wait()
-
+        at(1, nz // 2 - 1, met)
+        at(0, nz // 2 - 1, greet)
+        both(stage_d, 4, PICK_AT + 4)
         both(stage_e, LAG_E, SUM_AT)
 
         @pl.when(t == PICK_AT)
@@ -436,10 +458,11 @@
             drain(xi_buf.at[pl.ds(1, NX - 1)], xi_recv)
 
         at(PICK_AT, EARLY, early_pick)
+        at(2, groups, wait_sums)
+        at(1, groups - 2, lambda k: stage_a(k + 2))
+        at(2, first_early, stage_c)
         at(PICK_AT + 2, EARLY, early_sum)
-        at(2, first_early, stage_c)
         at(2 + first_early, EARLY, lambda e: early_end(first_early + e))
-        both(stage_d, 3, PICK_AT + 3)
         return carry
 
     lax.fori_loop(0, max(groups + 2, first_early + LAG_E, SUM_AT + EARLY), step, 0)
@@ -453,6 +476,19 @@
     drain(upd_v.at[:, : width // NC], u_recv)
     drain(y_buf.at[:, pl.ds(1, NY * NC - 1)], y_send)
     drain(z_buf.at[:, pl.ds(1, nz - 1)], z_send)
+
+
+def store(next_v, upd_v, next_hbm, upd_hbm, sem):
+    rows = next_v.shape[0] // PARTS
+    copies = [
+        pltpu.make_async_copy(src.at[pl.ds(p * rows, rows)], dst.at[pl.ds(p * rows, rows)], sem.at[i, p])
+        for p in range(PARTS)
+        for i, (src, dst) in enumerate(((next_v, next_hbm), (upd_v, upd_hbm)))
+    ]
+    for copy in copies:
+        copy.start()
+    for copy in copies:
+        copy.wait()
 
 
 def body(grad_parts, momentum, indices):
@@ -505,6 +541,7 @@
         dma((groups,)),
         dma,
         dma((groups,)),
+        pltpu.SemaphoreType.REGULAR((nz // 2 - 1,)),
     ]
     out = pltpu.VMEM((rows, width), F32)
     moment_next, update = pl.pallas_call(
@@ -517,6 +554,15 @@
             collective_id=0, has_side_effects=True, vmem_limit_bytes=56 * 1024 * 1024
         ),
     )(grad, mom, idx, jnp.asarray(tables()))
+    out = jax.ShapeDtypeStruct((rows, width), F32)
+    moment_next, update = pl.pallas_call(
+        store,
+        out_shape=(out, out),
+        in_specs=[any_space] * 2,
+        out_specs=(any_space, any_space),
+        scratch_shapes=[dma((2, PARTS))],
+        compiler_params=pltpu.CompilerParams(vmem_limit_bytes=1024 * 1024),
+    )(*(pltpu.with_memory_space_constraint(v, pltpu.VMEM) for v in (moment_next, update)))
     return (moment_next[None], update)
 
 

time: 80.9 us -> 75.5 us (0.933)
  Pallas kernels: 77.7 us -> 74.8 us
  local copies, waits for them, and re-layouts: 2.46 us -> 0 us
    pallas_call x1, Pallas kernels: 77.7 us -> 72.9 us  [body(): pl.pallas_call(functools.partial(kernel, groups), out_shape=(out, out), i...]
    unnamed x2 -> x0, local copies, waits for them, and re-layouts: 2.46 us -> none
    pallas_call x0 -> x1, Pallas kernels: none -> 1.85 us  [body(): pl.pallas_call(store, out_shape=(out, out), in_specs=[any_space] * 2, out...]
where the time goes in v4:
time: 75.5 us; the launch traced here: 75.4 us
  Pallas kernels  74.8 us (99%)
    pallas_call x1, Pallas kernels, body(): pl.pallas_call(functools.partial(kernel, groups), out_shape=(out, out), i...  72.9 us
    pallas_call x1, Pallas kernels, body(): pl.pallas_call(store, out_shape=(out, out), in_specs=[any_space] * 2, out...  1.85 us

profile of v4, /device:TPU:1, one launch (start us, length us, event | category | flops | bytes accessed | tf_op | source)
XLA Modules:
  0.0 75.4 jit_solution(5800423138141244998)
XLA Ops:
  0.6 72.9 %shard_map.59 = (f32[64,7168]{1,0:T(8,128)S(1)}, f32[64,7168]{1,0:T(8,128)S(1)}) custom-call(bf16[64,28672]{1,0:T(8,128)(2,1)} %bitcast.6, f32[64,7168]{1,0:T(8,128)} %bitcast.7, s32[64,32,112]{2,1,0:T(8,128)} %bitcast.8, bf16[1408,256]{1,0:T(8,128)(2,1)} %constant.2.clone.tab_hbm), custom_call_target="tpu_custom_call" | custom-call | tf_op jit(solution)/shard_map/pallas_call | solution.py:547
  73.6 1.9 %shard_map.60 = (f32[64,7168]{1,0:T(8,128)}, f32[64,7168]{1,0:T(8,128)}) custom-call(f32[64,7168]{1,0:T(8,128)S(1)} %get-tuple-element.6.next_v, f32[64,7168]{1,0:T(8,128)S(1)} %get-tuple-element.7.upd_v), custom_call_target="tpu_custom_call" | custom-call | tf_op jit(solution)/shard_map/pallas_call | solution.py:558

commit v5 on v4

--- a/solution.py
+++ b/solution.py
@@ -23,8 +23,8 @@
 PARTS = 1
 EARLY = 5
 HALF = BLOCKS // 2
-PICK_AT = 1
-SUM_AT = 10
+PICK_AT = 2
+SUM_AT = 9
 LAG_E = 6
 DECAY = 0.9
 
@@ -390,28 +390,28 @@
         )
     for where in (far, left, right_x):
         pl.semaphore_signal(barrier, inc=1, device_id=(rep, where), device_id_type=MESH)
+    start_loads(0)
     load_idx.start()
     load_tab.start()
-    start_loads(0)
-    for e in range(EARLY):
-        start_loads(first_early + e)
     start_loads(1)
-    load_idx.wait()
-
-    def turn_part(t, carry):
-        turn(t)
-        return carry
-
-    lax.fori_loop(0, nz // PREP, turn_part, 0)
-    xi_buf[0] = flat_v[0, c, first_early * BLOCKS :, :]
     wait_loads(0)
     widen(0)
-    load_tab.wait()
+    load_idx.wait()
+    turn(0)
+    xi_buf[0] = flat_v[0, c, first_early * BLOCKS :, :]
     pl.semaphore_wait(barrier, NX - 1 + NY * NC - 1 + 2)
     send_a(0)
     for s in range(1, NX):
         copy_xi(s).start()
     stage_a(1)
+    for e in range(EARLY):
+        start_loads(first_early + e)
+    def turn_part(t, carry):
+        turn(t)
+        return carry
+
+    lax.fori_loop(1, nz // PREP, turn_part, 0)
+    load_tab.wait()
     lax.fori_loop(0, EARLY, early_own, 0)
 
     def greet(t):

time: 75.5 us -> 74 us (0.980)
  Pallas kernels: 74.8 us -> 73.3 us
    pallas_call x1, Pallas kernels: 72.9 us -> 71.4 us  [body(): pl.pallas_call(functools.partial(kernel, groups), out_shape=(out, out), i...]
where the time goes in v5:
time: 74 us; the launch traced here: 73.9 us
  Pallas kernels  73.3 us (99%)
    pallas_call x1, Pallas kernels, body(): pl.pallas_call(functools.partial(kernel, groups), out_shape=(out, out), i...  71.4 us
    pallas_call x1, Pallas kernels, body(): pl.pallas_call(store, out_shape=(out, out), in_specs=[any_space] * 2, out...  1.85 us

profile of v5, /device:TPU:1, one launch (start us, length us, event | category | flops | bytes accessed | tf_op | source)
XLA Modules:
  0.0 73.9 jit_solution(3476168756349478190)
XLA Ops:
  0.6 71.4 %shard_map.59 = (f32[64,7168]{1,0:T(8,128)S(1)}, f32[64,7168]{1,0:T(8,128)S(1)}) custom-call(bf16[64,28672]{1,0:T(8,128)(2,1)} %bitcast.6, f32[64,7168]{1,0:T(8,128)} %bitcast.7, s32[64,32,112]{2,1,0:T(8,128)} %bitcast.8, bf16[1408,256]{1,0:T(8,128)(2,1)} %constant.2.clone.tab_hbm), custom_call_target="tpu_custom_call" | custom-call | tf_op jit(solution)/shard_map/pallas_call | solution.py:547
  72.0 1.9 %shard_map.60 = (f32[64,7168]{1,0:T(8,128)}, f32[64,7168]{1,0:T(8,128)}) custom-call(f32[64,7168]{1,0:T(8,128)S(1)} %get-tuple-element.6.next_v, f32[64,7168]{1,0:T(8,128)S(1)} %get-tuple-element.7.upd_v), custom_call_target="tpu_custom_call" | custom-call | tf_op jit(solution)/shard_map/pallas_call | solution.py:558

commit v6 on v5

--- a/solution.py
+++ b/solution.py
@@ -26,6 +26,7 @@
 PICK_AT = 2
 SUM_AT = 9
 LAG_E = 6
+FAR_FIRST = (4, 3, 5, 2, 6, 1, 7)
 DECAY = 0.9
 
 
@@ -281,7 +282,7 @@
         return DECAY * mom_v[g] + (grad_v[0, g].astype(F32) + (got[g, 0] + got[g, 1]))
 
     def send_y(g):
-        for step in range(1, NY * NC):
+        for step in FAR_FIRST:
             copy_y(g, step).start()
 
     def stage_c(g):
@@ -308,7 +309,7 @@
             copy_p(e, s).start()
             return carry
 
-        lax.fori_loop(1, NX, one_shard, 0, unroll=NX - 1)
+        lax.fori_loop(1, NX, one_shard, 0)
 
     def early_sum(e):
         g = first_early + e
@@ -330,8 +331,8 @@
             total = y_buf[g, same]
             for step in range(1, NY):
                 total += y_buf[g, same + NC * step]
-            z_buf[g, 0, core] = total
-        for step in range(1, nz):
+            z_buf[g, 0, core] = jnp.where(c == 0, total[:HALF], total[HALF:])
+        for step in FAR_FIRST:
             copy_z(g, step).start()
 
     def turn(t):
@@ -349,7 +350,7 @@
         k_buf[...] = flat >> 6
         l_buf[...] = flat & (SIDE - 1)
         drain(z_buf.at[g, pl.ds(1, nz - 1)], z_recv.at[g])
-        value = own_half(z_buf[g])
+        value = z_buf[g]
         high = value.astype(BF16).astype(F32)
         h_buf[...] = high
         w_buf[...] = value - high
@@ -516,7 +517,7 @@
         pltpu.VMEM((EARLY, NX - 1, BLOCKS, 128), F32),
         pltpu.VMEM((EARLY, NX, BLOCKS, 128), F32),
         pltpu.VMEM((groups, NY * NC, BLOCKS, 128), F32),
-        pltpu.VMEM((groups, nz, NC, BLOCKS, 128), F32),
+        pltpu.VMEM((groups, nz, NC, HALF, 128), F32),
         pltpu.VMEM((nz, NC, HALF, 128), I32),
         pltpu.VMEM((nz, NC, HALF, 128), I32),
         pltpu.VMEM((nz, NC, HALF, 128), F32),

time: 74 us -> 74 us (level)
  no operation moved by 1% of the time
where the time goes in v6:
time: 74 us; the launch traced here: 73.9 us
  Pallas kernels  73.3 us (99%)
    pallas_call x1, Pallas kernels, body(): pl.pallas_call(functools.partial(kernel, groups), out_shape=(out, out), i...  71.4 us
    pallas_call x1, Pallas kernels, body(): pl.pallas_call(store, out_shape=(out, out), in_specs=[any_space] * 2, out...  1.85 us

profile of v6, /device:TPU:1, one launch (start us, length us, event | category | flops | bytes accessed | tf_op | source)
XLA Modules:
  0.0 73.9 jit_solution(18300505200100958451)
XLA Ops:
  0.6 71.4 %shard_map.59 = (f32[64,7168]{1,0:T(8,128)S(1)}, f32[64,7168]{1,0:T(8,128)S(1)}) custom-call(bf16[64,28672]{1,0:T(8,128)(2,1)} %bitcast.6, f32[64,7168]{1,0:T(8,128)} %bitcast.7, s32[64,32,112]{2,1,0:T(8,128)} %bitcast.8, bf16[1408,256]{1,0:T(8,128)(2,1)} %constant.2.clone.tab_hbm), custom_call_target="tpu_custom_call" | custom-call | tf_op jit(solution)/shard_map/pallas_call | solution.py:548
  72.0 1.9 %shard_map.60 = (f32[64,7168]{1,0:T(8,128)}, f32[64,7168]{1,0:T(8,128)}) custom-call(f32[64,7168]{1,0:T(8,128)S(1)} %get-tuple-element.6.next_v, f32[64,7168]{1,0:T(8,128)S(1)} %get-tuple-element.7.upd_v), custom_call_target="tpu_custom_call" | custom-call | tf_op jit(solution)/shard_map/pallas_call | solution.py:559

commit v7 on v6

--- a/solution.py
+++ b/solution.py
@@ -181,8 +181,8 @@
     def copy_y(g, step):
         other = (place + step) % (NY * NC)
         return pltpu.make_async_remote_copy(
-            src_ref=y_buf.at[g, 0],
-            dst_ref=y_buf.at[g, NY * NC - step],
+            src_ref=y_buf.at[g, 0, other % NC],
+            dst_ref=y_buf.at[g, NY * NC - step, other % NC],
             send_sem=y_send,
             recv_sem=y_recv.at[g],
             device_id=(rep_of(z, other), x),
@@ -289,7 +289,7 @@
         taken, hit = places(own_rows(g))
         acc = summed(g)
         kept, column = pick(acc, taken, hit)
-        y_buf[g, 0] = as_rows(column)
+        y_buf[g, 0] = as_rows(column).reshape(NC, HALF, 128)
         send_y(g)
         next_v[:, columns(g)] = acc - put_back(kept, taken)
 
@@ -316,7 +316,7 @@
         taken, hit = places(own_rows(g))
         drain(p_got.at[e, pl.ds(1, NX - 1)], p_recv.at[e])
         rows = (p_got[e, 0] + p_got[e, 1]) + (p_got[e, 2] + p_got[e, 3])
-        y_buf[g, 0] = rows
+        y_buf[g, 0] = rows.reshape(NC, HALF, 128)
         send_y(g)
         kept = jnp.where(hit, as_column(rows, 0.0), 0.0)
         next_v[:, columns(g)] = put_back(kept, taken)
@@ -325,13 +325,13 @@
         next_v[:, columns(g)] = summed(g) - next_v[:, columns(g)]
 
     def stage_d(g):
-        drain(y_buf.at[g, pl.ds(1, NY * NC - 1)], y_recv.at[g])
+        drain(y_buf.at[g, pl.ds(1, NY * NC - 1), 0], y_recv.at[g])
         for core in range(NC):
             same = (core + NC - c) % NC
-            total = y_buf[g, same]
+            total = y_buf[g, same, c]
             for step in range(1, NY):
-                total += y_buf[g, same + NC * step]
-            z_buf[g, 0, core] = jnp.where(c == 0, total[:HALF], total[HALF:])
+                total += y_buf[g, same + NC * step, c]
+            z_buf[g, 0, core] = total
         for step in FAR_FIRST:
             copy_z(g, step).start()
 
@@ -475,7 +475,7 @@
     drain(p_own, p_send)
     drain(upd_v.at[:, : width // NC], u_send)
     drain(upd_v.at[:, : width // NC], u_recv)
-    drain(y_buf.at[:, pl.ds(1, NY * NC - 1)], y_send)
+    drain(y_buf.at[:, pl.ds(1, NY * NC - 1), 0], y_send)
     drain(z_buf.at[:, pl.ds(1, nz - 1)], z_send)
 
 
@@ -516,7 +516,7 @@
         pltpu.VMEM((NX, EARLY * BLOCKS, 128), I32),
         pltpu.VMEM((EARLY, NX - 1, BLOCKS, 128), F32),
         pltpu.VMEM((EARLY, NX, BLOCKS, 128), F32),
-        pltpu.VMEM((groups, NY * NC, BLOCKS, 128), F32),
+        pltpu.VMEM((groups, NY * NC, NC, HALF, 128), F32),
         pltpu.VMEM((groups, nz, NC, HALF, 128), F32),
         pltpu.VMEM((nz, NC, HALF, 128), I32),
         pltpu.VMEM((nz, NC, HALF, 128), I32),

time: 74 us -> 74 us (level)
  no operation moved by 1% of the time
where the time goes in v7:
time: 74 us; the launch traced here: 73.9 us
  Pallas kernels  73.3 us (99%)
    pallas_call x1, Pallas kernels, body(): pl.pallas_call(functools.partial(kernel, groups), out_shape=(out, out), i...  71.4 us
    pallas_call x1, Pallas kernels, body(): pl.pallas_call(store, out_shape=(out, out), in_specs=[any_space] * 2, out...  1.85 us

profile of v7, /device:TPU:1, one launch (start us, length us, event | category | flops | bytes accessed | tf_op | source)
XLA Modules:
  0.0 73.9 jit_solution(88150737415810597)
XLA Ops:
  0.6 71.4 %shard_map.59 = (f32[64,7168]{1,0:T(8,128)S(1)}, f32[64,7168]{1,0:T(8,128)S(1)}) custom-call(bf16[64,28672]{1,0:T(8,128)(2,1)} %bitcast.6, f32[64,7168]{1,0:T(8,128)} %bitcast.7, s32[64,32,112]{2,1,0:T(8,128)} %bitcast.8, bf16[1408,256]{1,0:T(8,128)(2,1)} %constant.2.clone.tab_hbm), custom_call_target="tpu_custom_call" | custom-call | tf_op jit(solution)/shard_map/pallas_call | solution.py:548
  72.0 1.9 %shard_map.60 = (f32[64,7168]{1,0:T(8,128)}, f32[64,7168]{1,0:T(8,128)}) custom-call(f32[64,7168]{1,0:T(8,128)S(1)} %get-tuple-element.6.next_v, f32[64,7168]{1,0:T(8,128)S(1)} %get-tuple-element.7.upd_v), custom_call_target="tpu_custom_call" | custom-call | tf_op jit(solution)/shard_map/pallas_call | solution.py:559
